TPU v7x, 32 devices: a whole 2x2x4 slice. The times are simulated.
32 devices in a mesh: dp: 8 (over y, x, core), seq: 4 (over z).
Axes of the slice: x: 2, y: 2, z: 4, core: 2. Of those that a mesh axis runs over, the one named last changes fastest.
Arguments:
- tokens: bfloat16 [8, 1024, 768], P('dp', 'seq'), may hold values from -6 to 6
- group_ids: int32 [8], P('dp'), may hold values from 0 to 15
- lengths: int32 [8], P('dp'), may hold values from 256 to 1024, as said below
- cotangent: bfloat16 [8, 1024, 768], P('dp', 'seq'), may hold values from -6 to 6
- group_table: float32 [16, 768], replicated, may hold values from -3 to 3
- first_gain: float32 [768], replicated, may hold values from 0.1 to 1.9
- first_shift: float32 [768], replicated, may hold values from -1.8 to 1.8
- qkv_weight: bfloat16 [768, 2304], replicated, may hold values from -0.21875 to 0.21875
- query_value_bias: float32 [2, 768], replicated, may hold values from -1.8 to 1.8
- out_weight: bfloat16 [768, 768], replicated, may hold values from -1.25 to 1.25
- out_bias: float32 [768], replicated, may hold values from -1.8 to 1.8
- second_gain: float32 [768], replicated, may hold values from 0.1 to 1.9
- second_shift: float32 [768], replicated, may hold values from -1.8 to 1.8
- up_weight: bfloat16 [768, 3072], replicated, may hold values from -0.21875 to 0.21875
- up_bias: float32 [3072], replicated, may hold values from -1.8 to 1.8
- down_weight: bfloat16 [3072, 768], replicated, may hold values from -0.109375 to 0.109375
- down_bias: float32 [768], replicated, may hold values from -1.8 to 1.8
Outputs:
- result: bfloat16 [8, 1024, 768], P('dp', 'seq')
- grad_tokens: bfloat16 [8, 1024, 768], P('dp', 'seq')
- grad_group_table: float32 [16, 768], replicated
- grad_first_gain: float32 [768], replicated
- grad_first_shift: float32 [768], replicated
- grad_qkv_weight: float32 [768, 2304], P('dp', 'seq')
- grad_query_value_bias: float32 [2, 768], replicated
- grad_out_weight: float32 [768, 768], P('dp', 'seq')
- grad_out_bias: float32 [768], replicated
- grad_second_gain: float32 [768], replicated
- grad_second_shift: float32 [768], replicated
- grad_up_weight: float32 [768, 3072], P('dp', 'seq')
- grad_up_bias: float32 [3072], replicated
- grad_down_weight: float32 [3072, 768], P('dp', 'seq')
- grad_down_bias: float32 [768], replicated
Inputs may be any that keep to these rules, and one draw needn't show every extreme that they name: `lengths`: in each index of dp (sequences k * 1 to k + 1 - 1) one sequence has length 1024.
All inputs are finite; a program needn't handle non-finite values.
Results may differ from a plain program's by a relative error of at most 0.015.
Values may be sent and summed in bfloat16 or wider, within the bound.
A program may use at most 128 MiB of HBM per device.

v0:
```python
import jax
import jax.numpy as jnp
from jax import lax
from jax.sharding import PartitionSpec as P

HEADS = 12
HEAD = 64


EPSILON = 1e-05
NEG_LARGE = -1e30
EXACT = lax.Precision.HIGHEST


def shifted(array, axis, by):
    devices = lax.axis_size(axis)
    pairs = [(i, i + by) for i in range(devices) if 0 <= i + by < devices]
    return lax.ppermute(array, axis, pairs)


def as_sent(array):
    return jax.tree.map(lambda a: a.astype(jnp.bfloat16) if a.dtype == jnp.float32 else a, array)


def shifted_2(block, axis, distance):
    devices = range(lax.axis_size(axis))
    route = [((i - distance) % len(devices), i) for i in devices]
    return lax.ppermute(block, axis, route)


def layer_norm(inputs, norm_gain, norm_shift):
    average = jnp.mean(inputs, -1, keepdims=True)
    centred = inputs - average
    inverse = lax.rsqrt(jnp.mean(centred * centred, -1, keepdims=True) + EPSILON)
    return centred * inverse * norm_gain + norm_shift


def tanh_gelu(inputs):
    return jax.nn.gelu(inputs, approximate=True)


def keep_same(state_value):
    return state_value


def scores_of(queries, key_piece, key_start, query_start, lengths):
    sequences, block_len = (queries.shape[0], queries.shape[1])
    key_heads = key_piece.reshape(sequences, key_piece.shape[1], HEADS, HEAD)
    raw_scores = jnp.einsum(
        "gqhe,gkhe->ghqk", queries, key_heads, preferred_element_type=jnp.float32
    ) * HEAD ** (-0.5)
    key_pos = key_start + jnp.arange(key_piece.shape[1])
    query_pos = query_start + jnp.arange(block_len)
    allowed = (query_pos[:, None] >= key_pos[None, :])[None] & (
        key_pos[None, None, :] < lengths[:, None, None]
    )
    return (raw_scores, allowed[:, None])


def shards(
    tokens,
    group_ids,
    lengths,
    cotangent,
    group_table,
    first_gain,
    first_shift,
    qkv_weight,
    query_value_bias,
    out_weight,
    out_bias,
    second_gain,
    second_shift,
    up_weight,
    up_bias,
    down_weight,
    down_bias,
):
    sequences, block_len, features = tokens.shape
    token_rows = sequences * block_len
    seq_count = lax.axis_size("seq")
    seq_index = lax.axis_index("seq")
    query_start = seq_index * block_len
    score_scale = HEAD ** (-0.5)
    one_hot = (group_ids[:, None] == jnp.arange(group_table.shape[0])[None, :]).astype(jnp.float32)
    table_rows = jnp.dot(one_hot, group_table, precision=EXACT)
    start_rows = (tokens.astype(jnp.float32) + table_rows[:, None, :]).reshape(token_rows, features)
    norm_one, pull_one = jax.vjp(layer_norm, start_rows, first_gain, first_shift)
    norm_one_low = norm_one.astype(jnp.bfloat16)
    full_bias = jnp.concatenate(
        [query_value_bias[0], jnp.zeros((features,), jnp.float32), query_value_bias[1]]
    )
    mixed_rows = (
        jnp.dot(norm_one_low, qkv_weight, preferred_element_type=jnp.float32) + full_bias
    ).astype(jnp.bfloat16)
    mixed_rows = mixed_rows.reshape(sequences, block_len, 3 * features)
    queries = mixed_rows[:, :, :features].reshape(sequences, block_len, HEADS, HEAD)
    key_rows = mixed_rows[:, :, features : 2 * features]
    values = mixed_rows[:, :, 2 * features :]
    pieces = []
    current = (key_rows, values)
    for cycle_step in range(seq_count):
        if cycle_step > 0:
            current = shifted((current[0], current[1]), "seq", 1)
        anchor = (seq_index - cycle_step) % seq_count
        pieces.append((current[0], current[1], anchor * block_len, cycle_step <= seq_index))
    shape_rows = (sequences, HEADS, block_len)
    row_max = jnp.full(shape_rows, NEG_LARGE, jnp.float32)
    row_sum = jnp.zeros(shape_rows, jnp.float32)
    stored = []
    for key_piece, value_piece, key_start, active in pieces:

        def visit_block(state_pair, key_piece=key_piece, key_start=key_start):
            raw_scores, allowed = scores_of(queries, key_piece, key_start, query_start, lengths)
            masked_scores = jnp.where(allowed, raw_scores, NEG_LARGE)
            new_max = jnp.maximum(state_pair[0], jnp.max(masked_scores, -1))
            weights = jnp.where(allowed, jnp.exp(masked_scores - new_max[..., None]), 0.0)
            return (
                new_max,
                state_pair[1] * jnp.exp(state_pair[0] - new_max) + jnp.sum(weights, -1),
                masked_scores,
            )

        def pass_block(state_pair):
            return (
                state_pair[0],
                state_pair[1],
                jnp.full(shape_rows + (block_len,), NEG_LARGE, jnp.float32),
            )

        row_max, row_sum, masked_scores = lax.cond(
            active, visit_block, pass_block, (row_max, row_sum)
        )
        stored.append(masked_scores)
    log_sum = row_max + jnp.log(row_sum)
    attended = jnp.zeros((sequences, block_len, HEADS, HEAD), jnp.float32)
    for piece_data, masked_scores in zip(pieces, stored):

        def attend_block(total_out, value_piece=piece_data[1], masked_scores=masked_scores):
            probs = jnp.exp(masked_scores - log_sum[..., None]).astype(jnp.bfloat16)
            value_heads = value_piece.reshape(sequences, block_len, HEADS, HEAD)
            return total_out + jnp.einsum(
                "ghqk,gkhe->gqhe", probs, value_heads, preferred_element_type=jnp.float32
            )

        attended = lax.cond(piece_data[3], attend_block, keep_same, attended)
    attended_low = attended.reshape(token_rows, features).astype(jnp.bfloat16)
    after_attn = (
        start_rows
        + jnp.dot(attended_low, out_weight, preferred_element_type=jnp.float32)
        + out_bias
    )
    norm_two, pull_two = jax.vjp(layer_norm, after_attn, second_gain, second_shift)
    norm_two_low = norm_two.astype(jnp.bfloat16)
    up_rows = jnp.dot(norm_two_low, up_weight, preferred_element_type=jnp.float32) + up_bias
    activated, pull_gelu = jax.vjp(tanh_gelu, up_rows)
    activated_low = activated.astype(jnp.bfloat16)
    result_rows = (
        after_attn
        + jnp.dot(activated_low, down_weight, preferred_element_type=jnp.float32)
        + down_bias
    )
    result = result_rows.astype(jnp.bfloat16).reshape(tokens.shape)
    outer_low = cotangent.reshape(token_rows, features)
    outer_grad = outer_low.astype(jnp.float32)
    grad_down_weight = jnp.dot(activated_low.T, outer_low, preferred_element_type=jnp.float32)
    grad_down_bias = jnp.sum(outer_grad, 0)
    up_grad = pull_gelu(jnp.dot(outer_low, down_weight.T, preferred_element_type=jnp.float32))[0]
    grad_up_bias = jnp.sum(up_grad, 0)
    up_low = up_grad.astype(jnp.bfloat16)
    grad_up_weight = jnp.dot(norm_two_low.T, up_low, preferred_element_type=jnp.float32)
    part_after, grad_second_gain, grad_second_shift = pull_two(
        jnp.dot(up_low, up_weight.T, preferred_element_type=jnp.float32)
    )
    after_grad = outer_grad + part_after
    grad_out_bias = jnp.sum(after_grad, 0)
    after_low = after_grad.astype(jnp.bfloat16)
    grad_out_weight = jnp.dot(attended_low.T, after_low, preferred_element_type=jnp.float32)
    out_grad = jnp.dot(after_low, out_weight.T, preferred_element_type=jnp.float32).astype(
        jnp.bfloat16
    )
    out_grad = out_grad.reshape(sequences, block_len, HEADS, HEAD)
    delta = jnp.transpose(jnp.sum(out_grad.astype(jnp.float32) * attended, -1), (0, 2, 1))

    def back_block(query_grad, key_piece, value_piece, key_start):
        raw_scores, allowed = scores_of(queries, key_piece, key_start, query_start, lengths)
        probs = jnp.where(allowed, jnp.exp(raw_scores - log_sum[..., None]), 0.0)
        value_heads = value_piece.reshape(sequences, block_len, HEADS, HEAD)
        key_heads = key_piece.reshape(sequences, block_len, HEADS, HEAD)
        prob_grad = jnp.einsum(
            "gqhe,gkhe->ghqk", out_grad, value_heads, preferred_element_type=jnp.float32
        )
        score_grad = (probs * (prob_grad - delta[..., None])).astype(jnp.bfloat16)
        query_grad = (
            query_grad
            + jnp.einsum(
                "ghqk,gkhe->gqhe", score_grad, key_heads, preferred_element_type=jnp.float32
            )
            * score_scale
        )
        key_add = (
            jnp.einsum("ghqk,gqhe->gkhe", score_grad, queries, preferred_element_type=jnp.float32)
            * score_scale
        )
        value_add = jnp.einsum(
            "ghqk,gqhe->gkhe",
            probs.astype(jnp.bfloat16),
            out_grad,
            preferred_element_type=jnp.float32,
        )
        return (
            query_grad,
            key_add.reshape(sequences, block_len, features),
            value_add.reshape(sequences, block_len, features),
        )

    empty_rows = jnp.zeros((sequences, block_len, features), jnp.float32)

    def skip_back(query_grad):
        return (query_grad, empty_rows, empty_rows)

    query_grad = jnp.zeros((sequences, block_len, HEADS, HEAD), jnp.float32)
    carried = (empty_rows, empty_rows)
    for cycle_step in range(seq_count):
        piece_data = pieces[cycle_step]

        def visit_back(state_grad, piece_data=piece_data):
            return back_block(state_grad, piece_data[0], piece_data[1], piece_data[2])

        query_grad, key_add, value_add = lax.cond(piece_data[3], visit_back, skip_back, query_grad)
        carried = shifted_2(
            (as_sent(carried[0] + key_add), as_sent(carried[1] + value_add)), "seq", 1
        )
    key_grad, value_grad = carried
    query_flat = query_grad.reshape(token_rows, features)
    key_flat = key_grad.reshape(token_rows, features)
    value_flat = value_grad.reshape(token_rows, features)
    grad_query_value_bias = jnp.stack([jnp.sum(query_flat, 0), jnp.sum(value_flat, 0)])
    mixed_grad = jnp.concatenate([query_flat, key_flat, value_flat], -1).astype(jnp.bfloat16)
    grad_qkv_weight = jnp.dot(norm_one_low.T, mixed_grad, preferred_element_type=jnp.float32)
    part_start, grad_first_gain, grad_first_shift = pull_one(
        jnp.dot(mixed_grad, qkv_weight.T, preferred_element_type=jnp.float32)
    )
    start_grad = after_grad + part_start
    grad_tokens = start_grad.astype(jnp.bfloat16).reshape(tokens.shape)
    grad_group_table = jnp.dot(
        one_hot.T, jnp.sum(start_grad.reshape(sequences, block_len, features), 1), precision=EXACT
    )
    small_sums = lax.psum(
        (
            grad_group_table,
            grad_first_gain,
            grad_first_shift,
            grad_query_value_bias,
            grad_out_bias,
            grad_second_gain,
            grad_second_shift,
            grad_up_bias,
            grad_down_bias,
        ),
        ("dp", "seq"),
    )
    matrices = (grad_qkv_weight, grad_out_weight, grad_up_weight, grad_down_weight)
    shares = (
        lax.psum_scatter(
            matrices[0].astype(jnp.bfloat16), "seq", scatter_dimension=1, tiled=True
        ).astype(jnp.float32),
        lax.psum_scatter(
            matrices[1].astype(jnp.bfloat16), "seq", scatter_dimension=1, tiled=True
        ).astype(jnp.float32),
        lax.psum_scatter(
            matrices[2].astype(jnp.bfloat16), "seq", scatter_dimension=1, tiled=True
        ).astype(jnp.float32),
        lax.psum_scatter(
            matrices[3].astype(jnp.bfloat16), "seq", scatter_dimension=1, tiled=True
        ).astype(jnp.float32),
    )
    shares = (
        lax.psum_scatter(
            shares[0].astype(jnp.bfloat16), "dp", scatter_dimension=0, tiled=True
        ).astype(jnp.float32),
        lax.psum_scatter(
            shares[1].astype(jnp.bfloat16), "dp", scatter_dimension=0, tiled=True
        ).astype(jnp.float32),
        lax.psum_scatter(
            shares[2].astype(jnp.bfloat16), "dp", scatter_dimension=0, tiled=True
        ).astype(jnp.float32),
        lax.psum_scatter(
            shares[3].astype(jnp.bfloat16), "dp", scatter_dimension=0, tiled=True
        ).astype(jnp.float32),
    )
    return (
        result,
        grad_tokens,
        small_sums[0],
        small_sums[1],
        small_sums[2],
        shares[0],
        small_sums[3],
        shares[1],
        small_sums[4],
        small_sums[5],
        small_sums[6],
        shares[2],
        small_sums[7],
        shares[3],
        small_sums[8],
    )


def solution(mesh):
    in_specs = (
        P("dp", "seq", None),
        P("dp"),
        P("dp"),
        P("dp", "seq", None),
        P(),
        P(),
        P(),
        P(),
        P(),
        P(),
        P(),
        P(),
        P(),
        P(),
        P(),
        P(),
        P(),
    )
    out_specs = (
        P("dp", "seq", None),
        P("dp", "seq", None),
        P(),
        P(),
        P(),
        P("dp", "seq"),
        P(),
        P("dp", "seq"),
        P(),
        P(),
        P(),
        P("dp", "seq"),
        P(),
        P("dp", "seq"),
        P(),
    )
    return jax.shard_map(shards, mesh=mesh, in_specs=in_specs, out_specs=out_specs, check_vma=False)
```

profile of v0, /device:TPU:0, one launch (start us, length us, event | category | flops | bytes accessed | tf_op | source)
XLA Modules:
  0.0 695.1 jit_solution(3165320408084809347)
XLA Ops:
  24.8 6.0 collective-permute-done
  47.6 5.3 collective-permute-start.2
  63.2 8.2 %conditional.12 = (f32[1,12,256]{2,1,0:T(8,128)S(1)}, f32[1,12,256]{2,1,0:T(8,128)}, f32[1,12,256,256]{2,3,1,0:T(8,128)}) conditional(s32[]{:T(128)} %convert_element_type.223, () %tuple.107, (s32[]{:T(128)}, s32[]{:T(128)}, s32[1]{0:T(128)}, bf16[1,256,12,64]{1,3,2,0:T(8,128)(2,1)}, bf16[1,256,768]{2,1,0:T(8,128)(2,1)}) %tuple.253), branch_computations={%region_2.3_spmd, %region_3.6_spmd} | conditional | flops 107096064 | bytes 11584068 | solution.py:131
  78.8 8.9 %conditional.16 = (f32[1,256,12,64]{1,3,2,0:T(8,128)}) conditional(s32[]{:T(128)} %convert_element_type.223, () %tuple.106, (f32[1,12,256]{2,1,0:T(8,128)}, f32[1,12,256,256]{2,3,1,0:T(8,128)}, bf16[1,256,768]{2,1,0:T(8,128)(2,1)}) %tuple.251), branch_computations={%region_18.19_spmd, %region_19.20_spmd} | conditional | flops 102236160 | bytes 11464740 | solution.py:146
  109.6 16.4 %conditional.20 = (f32[1,256,12,64]{1,3,2,0:T(8,128)}, bf16[1,256,768]{1,2,0:T(8,128)(2,1)}, bf16[1,256,768]{1,2,0:T(8,128)(2,1)}) conditional(s32[]{:T(128)} %convert_element_type.223, () %tuple.119, (s32[]{:T(128)}, s32[]{:T(128)}, s32[1]{0:T(128)}, bf16[1,256,12,64]{1,3,2,0:T(8,128)(2,1)}, bf16[1,256,768]{2,1,0:T(8,128)(2,1)}, ...), branch_computations={%region_31.32_spmd, %region_32.33_spmd} | conditional | flops 511902720 | bytes 37855924 | solution.py:230
  126.0 17.0 %collective-permute-start.6 = (bf16[1,256,768]{1,2,0:T(8,128)(2,1)}, bf16[1,256,768]{1,2,0:T(8,128)(2,1)}, u32[]{:S(2)}, u32[]{:S(2)}) collective-permute-start(bf16[1,256,768]{1,2,0:T(8,128)(2,1)} %get-tuple-element.337), channel_id=1, source_target_pairs={{3,0},{0,1},{1,2},{2,3},{7,4},{4,5},{5,6},{6,7},{11,8},{8,9},{9,10... | collective-permute-start | bytes 1179656 | tf_op jit(solution)/shard_map/ppermute | solution.py:28
  143.0 17.7 %collective-permute-start.10 = (bf16[1,256,768]{1,2,0:T(8,128)(2,1)}, bf16[1,256,768]{1,2,0:T(8,128)(2,1)}, u32[]{:S(2)}, u32[]{:S(2)}) collective-permute-start(bf16[1,256,768]{1,2,0:T(8,128)(2,1)} %get-tuple-element.341), channel_id=1, source_target_pairs={{3,0},{0,1},{1,2},{2,3},{7,4},{4,5},{5,6},{6,7},{11,8},{8,9},{9,10... | collective-permute-start | bytes 1179656 | tf_op jit(solution)/shard_map/ppermute | solution.py:28
  163.6 10.3 %conditional.21 = (f32[1,256,12,64]{1,3,2,0:T(8,128)}, f32[1,256,768]{1,2,0:T(8,128)}, f32[1,256,768]{1,2,0:T(8,128)}) conditional(s32[]{:T(128)} %convert_element_type.222, f32[1,256,12,64]{1,3,2,0:T(8,128)} %get-tuple-element.333, (s32[]{:T(128)}, s32[]{:T(128)}, s32[1]{0:T(128)}, bf16[1,256,12,64]{1,3,2,0:T(8,128)(2,1)}, ...), branch_computations={%region_33.34_spmd, %region_34.35_spmd} | conditional | flops 511902720 | bytes 39428788 | solution.py:230
  173.9 11.6 %collective-permute-done.6 = bf16[1,256,768]{1,2,0:T(8,128)(2,1)} collective-permute-done((bf16[1,256,768]{1,2,0:T(8,128)(2,1)}, bf16[1,256,768]{1,2,0:T(8,128)(2,1)}, u32[]{:S(2)}, u32[]{:S(2)}) %collective-permute-start.6) | collective-permute-done | bytes 393248 | tf_op jit(solution)/shard_map/ppermute | solution.py:28
  187.6 20.2 %collective-permute-start.7 = (bf16[1,256,768]{1,2,0:T(8,128)(2,1)}, bf16[1,256,768]{1,2,0:T(8,128)(2,1)}, u32[]{:S(2)}, u32[]{:S(2)}) collective-permute-start(bf16[1,256,768]{1,2,0:T(8,128)(2,1)} %add_convert_fusion.5), channel_id=1, source_target_pairs={{3,0},{0,1},{1,2},{2,3},{7,4},{4,5},{5,6},{6,7},{11,8},{8,9},{9,10... | collective-permute-start | bytes 1179656 | tf_op jit(solution)/shard_map/ppermute | solution.py:28
  211.8 7.6 %collective-permute-done.7 = bf16[1,256,768]{1,2,0:T(8,128)(2,1)} collective-permute-done((bf16[1,256,768]{1,2,0:T(8,128)(2,1)}, bf16[1,256,768]{1,2,0:T(8,128)(2,1)}, u32[]{:S(2)}, u32[]{:S(2)}) %collective-permute-start.7) | collective-permute-done | bytes 393248 | tf_op jit(solution)/shard_map/ppermute | solution.py:28
  228.9 7.4 %collective-permute-start.12 = (bf16[1,256,768]{1,2,0:T(8,128)(2,1)}, bf16[1,256,768]{1,2,0:T(8,128)(2,1)}, u32[]{:S(2)}, u32[]{:S(2)}) collective-permute-start(bf16[1,256,768]{1,2,0:T(8,128)(2,1)} %add_convert_fusion.1), channel_id=1, source_target_pairs={{3,0},{0,1},{1,2},{2,3},{7,4},{4,5},{5,6},{6,7},{11,8},{8,9},{9,10... | collective-permute-start | bytes 1179656 | tf_op jit(solution)/shard_map/ppermute | solution.py:28
  238.2 5.8 collective-permute-done.8
  254.2 10.8 %collective-permute-done.9 = bf16[1,256,768]{1,2,0:T(8,128)(2,1)S(1)} collective-permute-done((bf16[1,256,768]{1,2,0:T(8,128)(2,1)S(1)}, bf16[1,256,768]{1,2,0:T(8,128)(2,1)S(1)}, u32[]{:S(2)}, u32[]{:S(2)}) %collective-permute-start.9) | collective-permute-done | bytes 393248 | tf_op jit(solution)/shard_map/ppermute | solution.py:28
  273.4 5.7 convolution_convert_fusion.1
  279.8 5.4 convolution_convert_fusion.2
  287.3 51.9 %reduce-scatter.15.cloned.1.call-done = bf16[768,576]{0,1:T(8,128)(2,1)} async-done(((bf16[768,2304]{0,1:T(8,128)(2,1)}), bf16[768,576]{0,1:T(8,128)(2,1)}) %reduce-scatter.15.cloned.1.call-update) | async-done | bytes 884752 | tf_op jit(solution)/shard_map/reduce_scatter | solution.py:265
  341.5 85.7 %reduce-scatter.23.cloned.1.call-done = bf16[3072,192]{0,1:T(8,128)(2,1)} async-done(((bf16[3072,768]{0,1:T(8,128)(2,1)}), bf16[3072,192]{0,1:T(8,128)(2,1)}) %reduce-scatter.23.cloned.1.call-update) | async-done | bytes 1179664 | tf_op jit(solution)/shard_map/reduce_scatter | solution.py:274
  429.8 85.5 %reduce-scatter.19.cloned.1.call-done = bf16[768,768]{1,0:T(8,128)(2,1)} async-done(((bf16[768,3072]{1,0:T(8,128)(2,1)}), bf16[768,768]{1,0:T(8,128)(2,1)}) %reduce-scatter.19.cloned.1.call-update) | async-done | bytes 1179664 | tf_op jit(solution)/shard_map/reduce_scatter | solution.py:271
  523.9 6.2 fusion.128
  530.1 22.8 %reduce-scatter.27.cloned.1.call-done = bf16[96,192]{1,0:T(8,128)(2,1)} async-done(((bf16[768,192]{1,0:T(8,128)(2,1)}), bf16[96,192]{1,0:T(8,128)(2,1)}) %reduce-scatter.27.cloned.1.call-update) | async-done | bytes 36880
  556.0 36.1 %reduce-scatter.25.cloned.1.call-done = bf16[96,576]{1,0:T(8,128)(2,1)} async-done(((bf16[768,576]{1,0:T(8,128)(2,1)}), bf16[96,576]{1,0:T(8,128)(2,1)}) %reduce-scatter.25.cloned.1.call-update) | async-done | bytes 110608
  595.6 38.5 %reduce-scatter.29.cloned.1.call-done = bf16[384,192]{1,0:T(8,128)(2,1)} async-done(((bf16[3072,192]{1,0:T(8,128)(2,1)}), bf16[384,192]{1,0:T(8,128)(2,1)}) %reduce-scatter.29.cloned.1.call-update) | async-done | bytes 147472
  637.4 36.7 %reduce-scatter.21.cloned.1.call-done = bf16[96,768]{1,0:T(8,128)(2,1)} async-done(((bf16[768,768]{1,0:T(8,128)(2,1)}), bf16[96,768]{1,0:T(8,128)(2,1)}) %reduce-scatter.21.cloned.1.call-update) | async-done | bytes 147472 | tf_op jit(solution)/shard_map/reduce_scatter | solution.py:285
  (252 shorter events, 195.1 us)
Async XLA Ops:
  8.0 277.3 %reduce-scatter.17.cloned.1.call-start = ((), (), s32[]{:S(2)}) async-start(), calls=%async_computation.9 | async-start | bytes 1474560 | tf_op jit(solution)/shard_map/reduce_scatter | solution.py:268
  16.4 14.4 %collective-permute-start = (bf16[1,256,768]{2,1,0:T(8,128)(2,1)S(1)}, bf16[1,256,768]{2,1,0:T(8,128)(2,1)S(1)}, u32[]{:S(2)}, u32[]{:S(2)}) collective-permute-start(bf16[1,256,768]{2,1,0:T(8,128)(2,1)S(1)} %get-tuple-element.689), channel_id=1, source_target_pairs={{0,1},{1,2},{2,3},{4,5},{5,6},{6,7},{8,9},{9,10},{10,11},{12,13},{... | collective-permute-start | bytes 1179656 | tf_op jit(solution)/shard_map/ppermute | solution.py:18
  21.3 17.9 %collective-permute-start.3 = (bf16[1,256,768]{2,1,0:T(8,128)(2,1)S(1)}, bf16[1,256,768]{2,1,0:T(8,128)(2,1)S(1)}, u32[]{:S(2)}, u32[]{:S(2)}) collective-permute-start(bf16[1,256,768]{2,1,0:T(8,128)(2,1)S(1)} %get-tuple-element.688), channel_id=1, source_target_pairs={{0,1},{1,2},{2,3},{4,5},{5,6},{6,7},{8,9},{9,10},{10,11},{12,13},{... | collective-permute-start | bytes 1179656 | tf_op jit(solution)/shard_map/ppermute | solution.py:18
  30.8 16.9 %collective-permute-start.1 = (bf16[1,256,768]{2,1,0:T(8,128)(2,1)S(1)}, bf16[1,256,768]{2,1,0:T(8,128)(2,1)}, u32[]{:S(2)}, u32[]{:S(2)}) collective-permute-start(bf16[1,256,768]{2,1,0:T(8,128)(2,1)S(1)} %collective-permute-done), channel_id=1, source_target_pairs={{0,1},{1,2},{2,3},{4,5},{5,6},{6,7},{8,9},{9,10},{10,11},{12,13},{... | collective-permute-start | bytes 1179656 | tf_op jit(solution)/shard_map/ppermute | solution.py:18
  39.2 16.8 %collective-permute-start.4 = (bf16[1,256,768]{2,1,0:T(8,128)(2,1)S(1)}, bf16[1,256,768]{2,1,0:T(8,128)(2,1)}, u32[]{:S(2)}, u32[]{:S(2)}) collective-permute-start(bf16[1,256,768]{2,1,0:T(8,128)(2,1)S(1)} %collective-permute-done.3), channel_id=1, source_target_pairs={{0,1},{1,2},{2,3},{4,5},{5,6},{6,7},{8,9},{9,10},{10,11},{12,13},{... | collective-permute-start | bytes 1179656 | tf_op jit(solution)/shard_map/ppermute | solution.py:18
  47.6 27.9 %collective-permute-start.2 = (bf16[1,256,768]{2,1,0:T(8,128)(2,1)}, bf16[1,256,768]{2,1,0:T(8,128)(2,1)}, u32[]{:S(2)}, u32[]{:S(2)}) collective-permute-start(bf16[1,256,768]{2,1,0:T(8,128)(2,1)} %collective-permute-done.1), channel_id=1, source_target_pairs={{0,1},{1,2},{2,3},{4,5},{5,6},{6,7},{8,9},{9,10},{10,11},{12,13},{... | collective-permute-start | bytes 1179656 | tf_op jit(solution)/shard_map/ppermute | solution.py:18
  56.1 32.0 %collective-permute-start.5 = (bf16[1,256,768]{2,1,0:T(8,128)(2,1)}, bf16[1,256,768]{2,1,0:T(8,128)(2,1)}, u32[]{:S(2)}, u32[]{:S(2)}) collective-permute-start(bf16[1,256,768]{2,1,0:T(8,128)(2,1)} %collective-permute-done.4), channel_id=1, source_target_pairs={{0,1},{1,2},{2,3},{4,5},{5,6},{6,7},{8,9},{9,10},{10,11},{12,13},{... | collective-permute-start | bytes 1179656 | tf_op jit(solution)/shard_map/ppermute | solution.py:18
  126.0 59.5 %collective-permute-start.6 = (bf16[1,256,768]{1,2,0:T(8,128)(2,1)}, bf16[1,256,768]{1,2,0:T(8,128)(2,1)}, u32[]{:S(2)}, u32[]{:S(2)}) collective-permute-start(bf16[1,256,768]{1,2,0:T(8,128)(2,1)} %get-tuple-element.337), channel_id=1, source_target_pairs={{3,0},{0,1},{1,2},{2,3},{7,4},{4,5},{5,6},{6,7},{11,8},{8,9},{9,10... | collective-permute-start | bytes 1179656 | tf_op jit(solution)/shard_map/ppermute | solution.py:28
  143.0 64.8 %collective-permute-start.10 = (bf16[1,256,768]{1,2,0:T(8,128)(2,1)}, bf16[1,256,768]{1,2,0:T(8,128)(2,1)}, u32[]{:S(2)}, u32[]{:S(2)}) collective-permute-start(bf16[1,256,768]{1,2,0:T(8,128)(2,1)} %get-tuple-element.341), channel_id=1, source_target_pairs={{3,0},{0,1},{1,2},{2,3},{7,4},{4,5},{5,6},{6,7},{11,8},{8,9},{9,10... | collective-permute-start | bytes 1179656 | tf_op jit(solution)/shard_map/ppermute | solution.py:28
  163.5 175.7 %reduce-scatter.15.cloned.1.call-start = ((), (), s32[]{:S(2)}) async-start(), calls=%async_computation.8 | async-start | bytes 4423680 | tf_op jit(solution)/shard_map/reduce_scatter | solution.py:265
  187.6 31.8 %collective-permute-start.7 = (bf16[1,256,768]{1,2,0:T(8,128)(2,1)}, bf16[1,256,768]{1,2,0:T(8,128)(2,1)}, u32[]{:S(2)}, u32[]{:S(2)}) collective-permute-start(bf16[1,256,768]{1,2,0:T(8,128)(2,1)} %add_convert_fusion.5), channel_id=1, source_target_pairs={{3,0},{0,1},{1,2},{2,3},{7,4},{4,5},{5,6},{6,7},{11,8},{8,9},{9,10... | collective-permute-start | bytes 1179656 | tf_op jit(solution)/shard_map/ppermute | solution.py:28
  209.9 16.9 %collective-permute-start.11 = (bf16[1,256,768]{1,2,0:T(8,128)(2,1)}, bf16[1,256,768]{1,2,0:T(8,128)(2,1)}, u32[]{:S(2)}, u32[]{:S(2)}) collective-permute-start(bf16[1,256,768]{1,2,0:T(8,128)(2,1)} %add_convert_fusion.2), channel_id=1, source_target_pairs={{3,0},{0,1},{1,2},{2,3},{7,4},{4,5},{5,6},{6,7},{11,8},{8,9},{9,10... | collective-permute-start | bytes 1179656 | tf_op jit(solution)/shard_map/ppermute | solution.py:28
  221.4 22.5 %collective-permute-start.8 = (bf16[1,256,768]{1,2,0:T(8,128)(2,1)}, bf16[1,256,768]{1,2,0:T(8,128)(2,1)}, u32[]{:S(2)}, u32[]{:S(2)}) collective-permute-start(bf16[1,256,768]{1,2,0:T(8,128)(2,1)} %add_convert_fusion.4), channel_id=1, source_target_pairs={{3,0},{0,1},{1,2},{2,3},{7,4},{4,5},{5,6},{6,7},{11,8},{8,9},{9,10... | collective-permute-start | bytes 1179656 | tf_op jit(solution)/shard_map/ppermute | solution.py:28
  228.9 19.4 %collective-permute-start.12 = (bf16[1,256,768]{1,2,0:T(8,128)(2,1)}, bf16[1,256,768]{1,2,0:T(8,128)(2,1)}, u32[]{:S(2)}, u32[]{:S(2)}) collective-permute-start(bf16[1,256,768]{1,2,0:T(8,128)(2,1)} %add_convert_fusion.1), channel_id=1, source_target_pairs={{3,0},{0,1},{1,2},{2,3},{7,4},{4,5},{5,6},{6,7},{11,8},{8,9},{9,10... | collective-permute-start | bytes 1179656 | tf_op jit(solution)/shard_map/ppermute | solution.py:28
  245.3 19.7 %collective-permute-start.9 = (bf16[1,256,768]{1,2,0:T(8,128)(2,1)S(1)}, bf16[1,256,768]{1,2,0:T(8,128)(2,1)S(1)}, u32[]{:S(2)}, u32[]{:S(2)}) collective-permute-start(bf16[1,256,768]{1,2,0:T(8,128)(2,1)S(1)} %add_convert_fusion.3), channel_id=1, source_target_pairs={{3,0},{0,1},{1,2},{2,3},{7,4},{4,5},{5,6},{6,7},{11,8},{8,9},{9,10... | collective-permute-start | bytes 1179656 | tf_op jit(solution)/shard_map/ppermute | solution.py:28
  249.6 19.7 %collective-permute-start.13 = (bf16[1,256,768]{1,2,0:T(8,128)(2,1)S(1)}, bf16[1,256,768]{1,2,0:T(8,128)(2,1)S(1)}, u32[]{:S(2)}, u32[]{:S(2)}) collective-permute-start(bf16[1,256,768]{1,2,0:T(8,128)(2,1)S(1)} %add_convert_fusion), channel_id=1, source_target_pairs={{3,0},{0,1},{1,2},{2,3},{7,4},{4,5},{5,6},{6,7},{11,8},{8,9},{9,10... | collective-permute-start | bytes 1179656 | tf_op jit(solution)/shard_map/ppermute | solution.py:28
  273.3 153.9 %reduce-scatter.23.cloned.1.call-start = ((), (), s32[]{:S(2)}) async-start(), calls=%async_computation.12 | async-start | bytes 5898240 | tf_op jit(solution)/shard_map/reduce_scatter | solution.py:274
  279.1 236.2 %reduce-scatter.19.cloned.1.call-start = ((), (), s32[]{:S(2)}) async-start(), calls=%async_computation.10 | async-start | bytes 5898240 | tf_op jit(solution)/shard_map/reduce_scatter | solution.py:271
  285.3 267.7 %reduce-scatter.27.cloned.1.call-start = ((), (), s32[]{:S(2)}) async-start(), calls=%async_computation.14 | async-start | bytes 442368
  287.3 304.9 %reduce-scatter.25.cloned.1.call-start = ((), (), s32[]{:S(2)}) async-start(), calls=%async_computation.13 | async-start | bytes 1105920
  341.5 174.4 %copy-start.51 = (f32[12,64]{1,0:T(8,128)S(1)}, f32[12,64]{1,0:T(8,128)}, u32[]{:S(2)}) copy-start(f32[12,64]{1,0:T(8,128)} %get-tuple-element.691) | copy-start | bytes 9220
  341.5 292.6 %reduce-scatter.29.cloned.1.call-start = ((), (), s32[]{:S(2)}) async-start(), calls=%async_computation.15 | async-start | bytes 1769472
  429.8 244.3 %reduce-scatter.21.cloned.1.call-start = ((), (), s32[]{:S(2)}) async-start(), calls=%async_computation.11 | async-start | bytes 1327104 | tf_op jit(solution)/shard_map/reduce_scatter | solution.py:285
  515.3 160.4 %all-reduce.3.cloned.1.call-start = ((), (), s32[]{:S(2)}) async-start(), calls=%async_computation.16 | async-start | bytes 184320 | tf_op jit(solution)/shard_map/psum | solution.py:249
  (53 other events, 418.9 us)
Sparse Core Ops, SparseCore 0:
  163.6 50.1 reduce-scatter.16
  273.4 65.7 reduce-scatter.14
  341.6 85.5 reduce-scatter.22
  429.5 85.7 reduce-scatter.18
  518.5 34.4 reduce-scatter.26
  556.4 35.7 reduce-scatter.24
  595.4 38.5 reduce-scatter.28
  637.3 36.7 reduce-scatter.20
Sparse Core Ops, SparseCore 1:
  524.0 126.1 all-reduce.2
where the time goes:
time: 705 us; the launch traced here: 695 us
  waiting for transfers between devices  421 us (60%)
  starting transfers between devices  95.4 us (14%)
  matrix products  59.7 us (8%)
  local copies, waits for them, and re-layouts  58.1 us (8%)
  other arithmetic  35.2 us (5%)
  between operations  17.2 us (2%)
  loops' own time  8.78 us (1%)
    unnamed x12, waiting for transfers between devices  97.6 us
    reduce_scatter x1, waiting for transfers between devices, shards(): lax.psum_scatter(matrices[3].astype(jnp.bfloat16), 'seq', scatter_dimensi...  85.7 us
    reduce_scatter x1, waiting for transfers between devices, shards(): lax.psum_scatter(matrices[2].astype(jnp.bfloat16), 'seq', scatter_dimensi...  85.5 us
    ppermute x8, starting transfers between devices, shifted_2(): return lax.ppermute(block, axis, route)  65.9 us
    reduce_scatter x1, waiting for transfers between devices, shards(): lax.psum_scatter(matrices[0].astype(jnp.bfloat16), 'seq', scatter_dimensi...  51.9 us
    ppermute x8, waiting for transfers between devices, shifted_2(): return lax.ppermute(block, axis, route)  47.5 us
    reduce_scatter x1, waiting for transfers between devices, shards(): lax.psum_scatter(shares[2].astype(jnp.bfloat16), 'dp', scatter_dimension=...  36.7 us
    unnamed x111, local copies, waits for them, and re-layouts  29.7 us
  transfers between devices with their start and end apart: 23, of which 18 were waited for; matrix products, arithmetic and copies ran while one was open for 14% of the time, Pallas kernels for 0%

commit v1 on v0

--- a/solution.py
+++ b/solution.py
@@ -1,6 +1,12 @@
+import functools
+import math
+import types
+
 import jax
 import jax.numpy as jnp
 from jax import lax
+from jax.experimental import pallas as pl
+from jax.experimental.pallas import tpu as pltpu
 from jax.sharding import PartitionSpec as P
 
 HEADS = 12
@@ -10,6 +16,755 @@
 EPSILON = 1e-05
 NEG_LARGE = -1e30
 EXACT = lax.Precision.HIGHEST
+
+
+VMEM_LIMIT = 64 << 20
+
+
+BF = jnp.bfloat16
+F32 = jnp.float32
+MESH = pl.DeviceIdType.MESH
+LOG2E = 1.4426950408889634
+
+
+def dot(a, b):
+    return lax.dot_general(a, b, (((1,), (0,)), ((), ())), preferred_element_type=F32)
+
+
+def dot_nt(a, b):
+    return lax.dot_general(a, b, (((1,), (1,)), ((), ())), preferred_element_type=F32)
+
+
+def dot_tn(a, b):
+    return lax.dot_general(a, b, (((0,), (0,)), ((), ())), preferred_element_type=F32)
+
+
+def flipped(index, bit):
+    return index + bit - 2 * bit * lax.rem(index // bit, 2)
+
+
+class Place:
+    def __init__(self):
+        self.d = lax.axis_index("dp")
+        self.z = lax.axis_index("seq")
+        self.c = lax.rem(self.d, 2)
+        self.x = lax.rem(self.d // 2, 2)
+        self.y = lax.rem(self.d // 4, 2)
+        self.zl = lax.rem(self.z, 2)
+        self.zh = lax.rem(self.z // 2, 2)
+        self.core = (flipped(self.d, 1), self.z)
+        self.along_x = (flipped(self.d, 2), self.z)
+        self.along_y = (flipped(self.d, 4), self.z)
+        self.z_near = (self.d, flipped(self.z, 1))
+        self.z_far = (self.d, flipped(self.z, 2))
+
+    def around(self, k):
+        return (self.d, lax.rem(self.z + k, 4))
+
+
+def send(src, dst, sems, index, to):
+    copy = pltpu.make_async_remote_copy(
+        src_ref=src,
+        dst_ref=dst,
+        send_sem=sems.at[0, index],
+        recv_sem=sems.at[1, index],
+        device_id=to,
+        device_id_type=MESH,
+    )
+    return copy
+
+
+class ReduceScatter:
+    def __init__(self, place, g, rc, r1, r2, rz1, rz2, core_sems, sems, parts):
+        self.p, self.g, self.rc, self.r1, self.r2 = place, g, rc, r1, r2
+        self.rz1, self.rz2, self.core_sems, self.sems, self.parts = rz1, rz2, core_sems, sems, parts
+
+    def core_copy(self, part):
+        p = self.p
+        if self.parts == "yx":
+            ky, kx = part // 2, lax.rem(part, 2)
+            src = self.g.at[:, ky, kx, 1 - p.c]
+            dst = self.rc.at[:, ky, kx]
+        elif self.parts == "z":
+            kh, kl = part // 2, lax.rem(part, 2)
+            src = self.g.at[:, :, :, 1 - p.c, kh, kl]
+            dst = self.rc.at[:, :, :, kh, kl]
+        else:
+            src = self.g.at[:, :, :, 1 - p.c]
+            dst = self.rc
+        return send(src, dst, self.core_sems, part, p.core)
+
+    def core_start(self, part):
+        self.core_copy(part).start()
+
+    def core_sum(self):
+        p = self.p
+        for part in range(4 if self.parts else 1):
+            self.core_copy(part).wait()
+
+        def add(i, _):
+            h, ky, kx = i // 4, lax.rem(i // 2, 2), lax.rem(i, 2)
+            self.g[h, ky, kx, p.c] = self.g[h, ky, kx, p.c] + self.rc[h, ky, kx]
+            return 0
+
+        lax.fori_loop(0, 8, add, 0)
+
+    def first_copies(self):
+        p, g = self.p, self.g
+        return (
+            send(g.at[0, :, 1 - p.x, p.c], self.r1.at[0], self.sems, 0, p.along_x),
+            send(g.at[1, 1 - p.y, :, p.c], self.r1.at[1], self.sems, 1, p.along_y),
+        )
+
+    def first_start(self):
+        for copy in self.first_copies():
+            copy.start()
+
+    def first_sum(self):
+        p, g = self.p, self.g
+        for copy in self.first_copies():
+            copy.wait()
+        for i in range(2):
+            g[0, i, p.x, p.c] = g[0, i, p.x, p.c] + self.r1[0, i]
+            g[1, p.y, i, p.c] = g[1, p.y, i, p.c] + self.r1[1, i]
+
+    def second_copies(self):
+        p, g = self.p, self.g
+        return (
+            send(g.at[0, 1 - p.y, p.x, p.c], self.r2.at[0], self.sems, 2, p.along_y),
+            send(g.at[1, p.y, 1 - p.x, p.c], self.r2.at[1], self.sems, 3, p.along_x),
+        )
+
+    def second_start(self):
+        for copy in self.second_copies():
+            copy.start()
+
+    def second_sum(self):
+        p, g = self.p, self.g
+        for copy in self.second_copies():
+            copy.wait()
+        for h in range(2):
+            g[h, p.y, p.x, p.c] = g[h, p.y, p.x, p.c] + self.r2[h]
+
+    def third_copy(self):
+        p, g = self.p, self.g
+        return send(g.at[:, p.y, p.x, p.c, :, 1 - p.zl], self.rz1, self.sems, 4, p.z_near)
+
+    def third_start(self):
+        self.third_copy().start()
+
+    def third_sum(self):
+        p, g = self.p, self.g
+        self.third_copy().wait()
+        for h in range(2):
+            for i in range(2):
+                mine = (h, p.y, p.x, p.c, i, p.zl)
+                g[mine] = g[mine] + self.rz1[h, i]
+
+    def fourth_copy(self):
+        p, g = self.p, self.g
+        return send(g.at[:, p.y, p.x, p.c, 1 - p.zh, p.zl], self.rz2, self.sems, 5, p.z_far)
+
+    def fourth_start(self):
+        self.fourth_copy().start()
+
+    def fourth_sum(self, out):
+        p, g = self.p, self.g
+        self.fourth_copy().wait()
+        for h in range(2):
+            mine = (h, p.y, p.x, p.c, p.zh, p.zl)
+            out[h] = g[mine].astype(F32) + self.rz2[h].astype(F32)
+
+
+def norm_stats(v):
+    mean = jnp.mean(v, axis=-1, keepdims=True)
+    centred = v - mean
+    inverse = lax.rsqrt(jnp.mean(centred * centred, axis=-1, keepdims=True) + EPSILON)
+    return mean, inverse
+
+
+def norm_back(t, gain, n, inverse):
+    u = t * gain
+    return inverse * (
+        u - jnp.mean(u, axis=-1, keepdims=True) - n * jnp.mean(u * n, axis=-1, keepdims=True)
+    )
+
+
+def column_sum(v):
+    return jnp.sum(v, axis=0, keepdims=True)
+
+
+def layer_kernel(names, *refs):
+    r = types.SimpleNamespace(**dict(zip(names, refs)))
+    p = Place()
+    T, D = r.tokens.shape
+    U = HEADS // 4
+    HF = U * HEAD
+
+    barrier = pltpu.get_barrier_semaphore()
+    partners = [p.core, p.along_x, p.along_y] + [p.around(k) for k in (1, 2, 3)]
+    for partner in partners:
+        pl.semaphore_signal(barrier, inc=1, device_id=partner, device_id_type=MESH)
+
+    pool = r.pool
+    load_sems = r.load_sems
+
+    def load(src, dst, index):
+        copy = pltpu.make_async_copy(src, dst, load_sems.at[index])
+        copy.start()
+        return copy
+
+    tokens_load = load(r.tokens, r.tok, 0)
+    qkv_loads = [
+        load(r.qkv_weight.at[:, pl.ds(i * D, D)], pool.at[1 + i], 1 + i) for i in range(3)
+    ]
+    cot_load = load(r.cotangent, r.cot, 4)
+    out_load = load(r.out_weight, pool.at[0], 5)
+
+    gid = r.group_ids[0]
+    length = r.lengths[0]
+    table = r.group_table[...]
+    group_rows = lax.broadcasted_iota(jnp.int32, table.shape, 0)
+    table_row = jnp.sum(jnp.where(group_rows == gid, table, 0.0), axis=0, keepdims=True)
+    tokens_load.wait()
+    start = r.tok[...].astype(F32) + table_row
+    r.start[...] = start
+    mean, inverse = norm_stats(start)
+    norm_one = ((start - mean) * inverse * r.first_gain[...] + r.first_shift[...]).astype(BF)
+    r.norm_oneT[...] = norm_one.T
+    mix = r.mix
+    qv_bias = r.qv_bias
+    for i in range(3):
+        qkv_loads[i].wait()
+        rows = dot(norm_one, pool[1 + i])
+        if i != 1:
+            rows = rows + qv_bias[pl.ds(i // 2, 1), :]
+        mix[i] = rows.astype(BF).T
+    up_loads = [
+        load(r.up_weight.at[:, pl.ds(i * D, D)], pool.at[1 + i], 6 + i) for i in range(4)
+    ]
+    down_loads = [
+        load(r.down_weight.at[pl.ds(i * D, D), :], pool.at[5 + i], 10 + i) for i in range(4)
+    ]
+
+    pl.semaphore_wait(barrier, len(partners))
+
+    qkv = r.qkv
+
+    def unit_rows(s, u):
+        return pl.ds(pl.multiple_of((s * U + u) * HEAD, HEAD), HEAD)
+
+    def qkv_copy(k, u):
+        to = p.around(k)
+        return send(
+            mix.at[:, unit_rows(to[1], u), :], qkv.at[u, p.z], r.qkv_sems, u * 3 + k - 1, to
+        )
+
+    for u in range(U):
+        for k in (1, 2, 3):
+            qkv_copy(k, u).start()
+    own_qkv = []
+    for u in range(U):
+        copy = pltpu.make_async_copy(
+            mix.at[:, unit_rows(p.z, u), :], qkv.at[u, p.z], r.own_sems.at[u]
+        )
+        copy.start()
+        own_qkv.append(copy)
+
+    cot_load.wait()
+    cot = r.cot[...]
+    r.cotT[...] = cot.T
+
+    key_iota = lax.broadcasted_iota(jnp.int32, (T, T), 0)
+    query_iota = lax.broadcasted_iota(jnp.int32, (T, T), 1)
+    scale2 = HEAD**-0.5 * LOG2E
+
+    def masked(u, i, j):
+        scores = dot_tn(qkv[u, j, 1], qkv[u, i, 0]) * scale2
+        allowed = key_iota < length - j * T
+        if i == j:
+            allowed = allowed & (key_iota <= query_iota)
+        return jnp.where(allowed, scores, NEG_LARGE)
+
+    attT, outT, out_low, lse = r.attT, r.outT, r.out_low, r.lse
+
+    def att_copy(k, u):
+        to = p.around(k)
+        return send(
+            out_low.at[u, to[1]],
+            attT.at[unit_rows(p.z, u), :],
+            r.att_sems,
+            u * 3 + k - 1,
+            to,
+        )
+
+    own_att = []
+    for u in range(U):
+        own_qkv[u].wait()
+        for k in (1, 2, 3):
+            qkv_copy(k, u).wait()
+        for i in range(4):
+            blocks = [masked(u, i, j) for j in range(i + 1)]
+            top = functools.reduce(
+                jnp.maximum, [jnp.max(b, axis=0, keepdims=True) for b in blocks]
+            )
+            weights = [jnp.exp2(b - top) for b in blocks]
+            total = sum(jnp.sum(w, axis=0, keepdims=True) for w in weights)
+            acc = sum(dot(qkv[u, j, 2], weights[j].astype(BF)) for j in range(i + 1))
+            value = acc * (1.0 / total)
+            outT[u, i] = value
+            out_low[u, i] = value.astype(BF)
+            lse[u, i] = top + jnp.log2(total)
+        for k in (1, 2, 3):
+            att_copy(k, u).start()
+        copy = pltpu.make_async_copy(
+            out_low.at[u, p.z], attT.at[unit_rows(p.z, u), :], r.own_sems.at[U + u]
+        )
+        copy.start()
+        own_att.append(copy)
+    for u in range(U):
+        own_att[u].wait()
+        for k in (1, 2, 3):
+            att_copy(k, u).wait()
+
+    out_load.wait()
+    after = start_of(r) + dot(attT[...].T, pool[0]) + r.out_bias[...]
+    r.after[...] = after
+    mean, inverse = norm_stats(after)
+    norm_two = ((after - mean) * inverse * r.second_gain[...] + r.second_shift[...]).astype(BF)
+    r.norm_two[...] = norm_two
+    r.norm_twoT[...] = norm_two.T
+    r.total[...] = after + r.down_bias[...]
+    r.t[...] = jnp.zeros((T, D), F32)
+    for copy in up_loads + down_loads:
+        copy.wait()
+
+    g_down, g_up, g_out, g_qkv = r.g_down, r.g_up, r.g_out, r.g_qkv
+
+    def scatter(name, parts):
+        return ReduceScatter(
+            p,
+            getattr(r, "g_" + name),
+            getattr(r, "rc_" + name),
+            getattr(r, "r1_" + name),
+            getattr(r, "r2_" + name),
+            getattr(r, "rz1_" + name),
+            getattr(r, "rz2_" + name),
+            getattr(r, "cs_" + name),
+            getattr(r, "ss_" + name),
+            parts,
+        )
+
+    down = scatter("down", "yx")
+    up = scatter("up", "z")
+    out = scatter("out", "")
+    proj = scatter("qkv", "")
+    small = r.small
+    gelu_c = math.sqrt(2.0 / math.pi)
+
+    def chunk(k, _):
+        kh, kl = k // 2, lax.rem(k, 2)
+        weight = pool[1 + k]
+        weight_down = pool[5 + k]
+        hidden = dot(r.norm_two[...], weight) + r.up_bias[pl.ds(k, 1), :]
+        act_grad = dot_nt(r.cot[...], weight_down)
+        square = hidden * hidden
+        th = jnp.tanh(gelu_c * hidden * (1.0 + 0.044715 * square))
+        half = 0.5 + 0.5 * th
+        act = (hidden * half).astype(BF)
+        slope = half + 0.5 * hidden * (1.0 - th * th) * gelu_c * (1.0 + 3 * 0.044715 * square)
+        grad = act_grad * slope
+        small[pl.ds(24 + k, 1), :] = column_sum(grad)
+        low = grad.astype(BF)
+        r.total[...] += dot(act, weight_down)
+        r.t[...] += dot_nt(low, weight)
+        piece = D // 2
+        for cc in range(2):
+            rows = dot(r.cotT[...], act[:, cc * piece : (cc + 1) * piece]).astype(BF)
+            part = D // 4
+            for z in range(4):
+                for h in range(2):
+                    at = z * part + h * (part // 2)
+                    g_down[h, kh, kl, cc, z // 2, z % 2] = rows[at : at + part // 2]
+        down.core_start(k)
+        rows = dot(r.norm_twoT[...], low).astype(BF)
+        part = D // 8
+        for d in range(8):
+            for h in range(2):
+                at = d * part + h * (part // 2)
+                g_up[h, d // 4, (d // 2) % 2, d % 2, kh, kl] = rows[at : at + part // 2]
+        up.core_start(k)
+        return 0
+
+    lax.fori_loop(0, 4, chunk, 0)
+
+    qkv_loads = [
+        load(r.qkv_weight.at[:, pl.ds(i * D, D)], pool.at[1 + i], 14 + i) for i in range(3)
+    ]
+
+    r.result[...] = r.total[...].astype(BF)
+    cot = r.cot[...].astype(F32)
+    after = r.after[...]
+    mean, inverse = norm_stats(after)
+    n = (after - mean) * inverse
+    t = r.t[...]
+    after_grad = cot + norm_back(t, r.second_gain[...], n, inverse)
+    r.after_grad[...] = after_grad
+    after_low = after_grad.astype(BF)
+    doT, dor = r.doT, r.dor
+    doT[...] = dot_nt(pool[0], after_low).astype(BF)
+
+    def do_copy(k):
+        to = p.around(k)
+        rows = pl.ds(pl.multiple_of(to[1] * HF, HF), HF)
+        return send(doT.at[rows, :], dor.at[p.z], r.do_sems, k - 1, to)
+
+    for k in (1, 2, 3):
+        do_copy(k).start()
+    own_do = pltpu.make_async_copy(
+        doT.at[pl.ds(pl.multiple_of(p.z * HF, HF), HF), :], dor.at[p.z], r.own_sems.at[2 * U]
+    )
+    own_do.start()
+    small[pl.ds(20, 1), :] = column_sum(after_grad)
+    small[pl.ds(21, 1), :] = column_sum(t * n)
+    small[pl.ds(22, 1), :] = column_sum(t)
+    small[pl.ds(23, 1), :] = column_sum(cot)
+    after_lowT = after_low.T
+    part = D // 8
+    for z in range(4):
+        rows = dot_nt(attT[...], after_lowT[z * (D // 4) : (z + 1) * (D // 4)]).astype(BF)
+        for d in range(8):
+            for h in range(2):
+                at = d * part + h * (part // 2)
+                g_out[h, d // 4, (d // 2) % 2, d % 2, z // 2, z % 2] = rows[at : at + part // 2]
+    out.core_start(0)
+
+    down.core_sum()
+    down.first_start()
+    up.core_sum()
+    up.first_start()
+    out.core_sum()
+    out.first_start()
+
+    own_do.wait()
+    for k in (1, 2, 3):
+        do_copy(k).wait()
+    mgT = r.mgT
+
+    def back_copy(k, u):
+        to = p.around(k)
+        return send(
+            mix.at[:, unit_rows(to[1], u), :],
+            mgT.at[:, unit_rows(p.z, u), :],
+            r.back_sems,
+            u * 3 + k - 1,
+            to,
+        )
+
+    own_back = []
+    for u in range(U):
+        key_grads = [jnp.zeros((HEAD, T), F32) for _ in range(4)]
+        value_grads = [jnp.zeros((HEAD, T), F32) for _ in range(4)]
+        for i in range(4):
+            do_i = dor[i, u * HEAD : (u + 1) * HEAD]
+            delta = column_sum(do_i.astype(F32) * outT[u, i])
+            lse_i = lse[u, i]
+            query_grad = jnp.zeros((HEAD, T), F32)
+            for j in range(i + 1):
+                probs = jnp.exp2(masked(u, i, j) - lse_i)
+                prob_grad = dot_tn(qkv[u, j, 2], do_i)
+                score_grad = (probs * (prob_grad - delta)).astype(BF)
+                query_grad += dot(qkv[u, j, 1], score_grad)
+                key_grads[j] += dot_nt(qkv[u, i, 0], score_grad)
+                value_grads[j] += dot_nt(do_i, probs.astype(BF))
+            mix[0, (i * U + u) * HEAD : (i * U + u + 1) * HEAD] = (query_grad * HEAD**-0.5).astype(BF)
+        for j in range(4):
+            rows = slice((j * U + u) * HEAD, (j * U + u + 1) * HEAD)
+            mix[1, rows] = (key_grads[j] * HEAD**-0.5).astype(BF)
+            mix[2, rows] = value_grads[j].astype(BF)
+        for k in (1, 2, 3):
+            back_copy(k, u).start()
+        copy = pltpu.make_async_copy(
+            mix.at[:, unit_rows(p.z, u), :],
+            mgT.at[:, unit_rows(p.z, u), :],
+            r.own_sems.at[2 * U + 1 + u],
+        )
+        copy.start()
+        own_back.append(copy)
+        if u == 1:
+            down.first_sum()
+            down.second_start()
+    up.first_sum()
+    up.second_start()
+    out.first_sum()
+    out.second_start()
+    down.second_sum()
+    down.third_start()
+    up.second_sum()
+    up.third_start()
+    out.second_sum()
+    out.third_start()
+
+    for u in range(U):
+        own_back[u].wait()
+        for k in (1, 2, 3):
+            back_copy(k, u).wait()
+
+    share = 3 * D // 4
+    part = D // 8
+    for z in range(4):
+        a, b = z * share // D, (z + 1) * share // D
+        cut = (z + 1) * share - b * D
+        pieces = [mgT[a, z * share - a * D : (D if b > a else cut)]]
+        if b > a and cut > 0:
+            pieces.append(mgT[b, 0:cut])
+        pieces = pieces[0] if len(pieces) == 1 else jnp.concatenate(pieces, axis=0)
+        rows = dot_nt(r.norm_oneT[...], pieces).astype(BF)
+        for d in range(8):
+            for h in range(2):
+                at = d * part + h * (part // 2)
+                g_qkv[h, d // 4, (d // 2) % 2, d % 2, z // 2, z % 2] = rows[at : at + part // 2]
+    proj.core_start(0)
+    for copy in qkv_loads:
+        copy.wait()
+    t1 = dot(pool[1], mgT[0]) + dot(pool[2], mgT[1]) + dot(pool[3], mgT[2])
+    t1 = t1.T
+    start = r.start[...]
+    mean, inverse = norm_stats(start)
+    n = (start - mean) * inverse
+    start_grad = r.after_grad[...] + norm_back(t1, r.first_gain[...], n, inverse)
+    r.grad_tokens[...] = start_grad.astype(BF)
+    ones = jnp.ones((8, T), BF)
+    small[pl.ds(0, 16), :] = jnp.where(group_rows == gid, column_sum(start_grad), 0.0)
+    small[pl.ds(16, 1), :] = column_sum(t1 * n)
+    small[pl.ds(17, 1), :] = column_sum(t1)
+    small[pl.ds(18, 1), :] = dot_nt(ones, mgT[0])[0:1]
+    small[pl.ds(19, 1), :] = dot_nt(ones, mgT[2])[0:1]
+
+    small_in, small_sems = r.small_in, r.small_sems
+    small_to = [p.core, p.along_x, p.along_y, p.z_near, p.z_far]
+
+    def small_copy(step):
+        return send(small, small_in.at[step], small_sems, step, small_to[step])
+
+    def small_sum(step):
+        small_copy(step).wait()
+        small[...] = small[...] + small_in[step]
+
+    small_copy(0).start()
+    proj.core_sum()
+    proj.first_start()
+    small_sum(0)
+    small_copy(1).start()
+    down.third_sum()
+    down.fourth_start()
+    up.third_sum()
+    up.fourth_start()
+    out.third_sum()
+    out.fourth_start()
+    small_sum(1)
+    small_copy(2).start()
+    proj.first_sum()
+    proj.second_start()
+    small_sum(2)
+    small_copy(3).start()
+    down.fourth_sum(r.s_down)
+    up.fourth_sum(r.s_up)
+    out.fourth_sum(r.s_out)
+    proj.second_sum()
+    proj.third_start()
+    small_sum(3)
+    small_copy(4).start()
+    proj.third_sum()
+    proj.fourth_start()
+    small_sum(4)
+    r.small_out[...] = small[...]
+    proj.fourth_sum(r.s_qkv)
+
+
+def start_of(r):
+    return r.start[...]
+
+
+def outputs_kernel(result, grad_tokens, small, s_qkv, s_out, s_up, s_down, *outs):
+    (
+        o_result,
+        o_tokens,
+        o_table,
+        o_first_gain,
+        o_first_shift,
+        o_qkv,
+        o_qv_bias,
+        o_out,
+        o_out_bias,
+        o_second_gain,
+        o_second_shift,
+        o_up,
+        o_up_bias,
+        o_down,
+        o_down_bias,
+    ) = outs
+    D = small.shape[1]
+    o_result[...] = result[...].reshape(o_result.shape)
+    o_tokens[...] = grad_tokens[...].reshape(o_tokens.shape)
+    o_table[...] = small[0:16]
+    o_qv_bias[...] = small[18:20]
+    for ref, row in (
+        (o_first_gain, 16),
+        (o_first_shift, 17),
+        (o_out_bias, 20),
+        (o_second_gain, 21),
+        (o_second_shift, 22),
+        (o_down_bias, 23),
+    ):
+        ref[...] = small[row]
+    for k in range(4):
+        o_up_bias[pl.ds(k * D, D)] = small[24 + k]
+    for ref, value in ((o_qkv, s_qkv), (o_out, s_out), (o_up, s_up)):
+        half = value.shape[1]
+        for h in range(2):
+            ref[h * half : (h + 1) * half] = value[h]
+    half = s_down.shape[1]
+    o_down[...] = jnp.concatenate([s_down[0], s_down[1]], axis=0).T
+
+
+def fused(
+    tokens,
+    group_ids,
+    lengths,
+    cotangent,
+    group_table,
+    first_gain,
+    first_shift,
+    qkv_weight,
+    query_value_bias,
+    out_weight,
+    out_bias,
+    second_gain,
+    second_shift,
+    up_weight,
+    up_bias,
+    down_weight,
+    down_bias,
+):
+    _, T, D = tokens.shape
+    F = up_weight.shape[1]
+    U = HEADS // 4
+    any_spec = pl.BlockSpec(memory_space=pl.ANY)
+    vmem = pl.BlockSpec(memory_space=pltpu.VMEM)
+    smem = pl.BlockSpec(memory_space=pltpu.SMEM)
+    inputs = dict(
+        tokens=(tokens.reshape(T, D), any_spec),
+        group_ids=(group_ids, smem),
+        lengths=(lengths, smem),
+        cotangent=(cotangent.reshape(T, D), any_spec),
+        group_table=(group_table, vmem),
+        first_gain=(first_gain.reshape(1, D), vmem),
+        first_shift=(first_shift.reshape(1, D), vmem),
+        qkv_weight=(qkv_weight, any_spec),
+        qv_bias=(query_value_bias, vmem),
+        out_weight=(out_weight, any_spec),
+        out_bias=(out_bias.reshape(1, D), vmem),
+        second_gain=(second_gain.reshape(1, D), vmem),
+        second_shift=(second_shift.reshape(1, D), vmem),
+        up_weight=(up_weight, any_spec),
+        up_bias=(up_bias.reshape(4, D), vmem),
+        down_weight=(down_weight, any_spec),
+        down_bias=(down_bias.reshape(1, D), vmem),
+    )
+    shares = dict(
+        down=(D // 8, F // 8),
+        up=(D // 16, F // 4),
+        out=(D // 16, D // 4),
+        qkv=(D // 16, 3 * D // 4),
+    )
+    outputs = dict(
+        result=((T, D), BF),
+        grad_tokens=((T, D), BF),
+        small_out=((28, D), F32),
+    )
+    outputs.update({"s_" + k: ((2,) + shares[k], F32) for k in ("qkv", "out", "up", "down")})
+    dma = pltpu.SemaphoreType.DMA
+    scratch = dict(
+        pool=pltpu.VMEM((9, D, D), BF),
+        tok=pltpu.VMEM((T, D), BF),
+        cot=pltpu.VMEM((T, D), BF),
+        cotT=pltpu.VMEM((D, T), BF),
+        start=pltpu.VMEM((T, D), F32),
+        norm_oneT=pltpu.VMEM((D, T), BF),
+        mix=pltpu.VMEM((3, D, T), BF),
+        qkv=pltpu.VMEM((U, 4, 3, HEAD, T), BF),
+        outT=pltpu.VMEM((U, 4, HEAD, T), F32),
+        out_low=pltpu.VMEM((U, 4, HEAD, T), BF),
+        lse=pltpu.VMEM((U, 4, 1, T), F32),
+        attT=pltpu.VMEM((D, T), BF),
+        after=pltpu.VMEM((T, D), F32),
+        norm_two=pltpu.VMEM((T, D), BF),
+        norm_twoT=pltpu.VMEM((D, T), BF),
+        total=pltpu.VMEM((T, D), F32),
+        t=pltpu.VMEM((T, D), F32),
+        after_grad=pltpu.VMEM((T, D), F32),
+        doT=pltpu.VMEM((D, T), BF),
+        dor=pltpu.VMEM((4, U * HEAD, T), BF),
+        mgT=pltpu.VMEM((3, D, T), BF),
+        small=pltpu.VMEM((28, D), F32),
+        small_in=pltpu.VMEM((5, 28, D), F32),
+        load_sems=dma((17,)),
+        own_sems=dma((3 * U + 1,)),
+        qkv_sems=dma((2, 3 * U)),
+        att_sems=dma((2, 3 * U)),
+        do_sems=dma((2, 3)),
+        back_sems=dma((2, 3 * U)),
+        small_sems=dma((2, 5)),
+    )
+    for name, (rows, columns) in shares.items():
+        extra = {
+            "g_" + name: pltpu.VMEM((2, 2, 2, 2, 2, 2, rows, columns), BF),
+            "rc_" + name: pltpu.VMEM((2, 2, 2, 2, 2, rows, columns), BF),
+            "r1_" + name: pltpu.VMEM((2, 2, 2, 2, rows, columns), BF),
+            "r2_" + name: pltpu.VMEM((2, 2, 2, rows, columns), BF),
+            "rz1_" + name: pltpu.VMEM((2, 2, rows, columns), BF),
+            "rz2_" + name: pltpu.VMEM((2, rows, columns), BF),
+            "cs_" + name: dma((2, 4)),
+            "ss_" + name: dma((2, 6)),
+        }
+        scratch.update(extra)
+    names = list(inputs) + list(outputs) + list(scratch)
+    done = pl.pallas_call(
+        functools.partial(layer_kernel, names),
+        name="layer",
+        out_shape=[jax.ShapeDtypeStruct(*o) for o in outputs.values()],
+        in_specs=[i[1] for i in inputs.values()],
+        out_specs=[vmem] * len(outputs),
+        scratch_shapes=list(scratch.values()),
+        compiler_params=pltpu.CompilerParams(
+            collective_id=0, has_side_effects=True, vmem_limit_bytes=VMEM_LIMIT
+        ),
+    )(*[i[0] for i in inputs.values()])
+    shape = jax.ShapeDtypeStruct
+    return pl.pallas_call(
+        outputs_kernel,
+        name="outputs",
+        out_shape=[
+            shape((1, T, D), BF),
+            shape((1, T, D), BF),
+            shape((16, D), F32),
+            shape((D,), F32),
+            shape((D,), F32),
+            shape((D // 8, 3 * D // 4), F32),
+            shape((2, D), F32),
+            shape((D // 8, D // 4), F32),
+            shape((D,), F32),
+            shape((D,), F32),
+            shape((D,), F32),
+            shape((D // 8, F // 4), F32),
+            shape((F,), F32),
+            shape((F // 8, D // 4), F32),
+            shape((D,), F32),
+        ],
+        in_specs=[vmem] * len(done),
+        out_specs=[vmem] * 15,
+    )(*done)
 
 
 def shifted(array, axis, by):
@@ -57,7 +812,7 @@
     return (raw_scores, allowed[:, None])
 
 
-def shards(
+def plain(
     tokens,
     group_ids,
     lengths,
@@ -345,4 +1100,8 @@
         P("dp", "seq"),
         P(),
     )
+    def shards(*arrays):
+        sizes = (mesh.shape["dp"], mesh.shape["seq"]) + arrays[0].shape
+        return (fused if sizes == (8, 4, 1, 256, 768) else plain)(*arrays)
+
     return jax.shard_map(shards, mesh=mesh, in_specs=in_specs, out_specs=out_specs, check_vma=False)

time: 705 us -> 165 us (0.23); the launches traced: 695 us -> 165 us
  waiting for transfers between devices: 421 us -> 0 us
  Pallas kernels: 0 us -> 152 us
  starting transfers between devices: 95.4 us -> 0 us
  matrix products: 59.7 us -> 0 us
  local copies, waits for them, and re-layouts: 58.1 us -> 10.8 us
  other arithmetic: 35.2 us -> 0 us
  between operations: 17.2 us -> 1.95 us
  loops' own time: 8.78 us -> 0 us
    reduce_scatter x5 -> x0, waiting for transfers between devices: 260 us -> none  [the longest x1 85.7 us: shards(): lax.psum_scatter(matrices[3].astype(jnp.bfloat16), 'seq', scatter_dimensi...]
    pallas_call x0 -> x2, Pallas kernels: none -> 152 us  [the longest x1 149 us: fused(): pl.pallas_call(functools.partial(layer_kernel, names), name='layer', out_...]
    unnamed x12 -> x0, waiting for transfers between devices: 97.6 us -> none
    ppermute x14 -> x0, starting transfers between devices: 95.1 us -> none  [the longest x8 65.9 us: shifted_2(): return lax.ppermute(block, axis, route)]
    ppermute x14 -> x0, waiting for transfers between devices: 63.2 us -> none  [the longest x8 47.5 us: shifted_2(): return lax.ppermute(block, axis, route)]
    dot_general x20 -> x0, matrix products: 59.7 us -> none  [the longest x1 6.23 us: shards(): jnp.dot(activated_low, down_weight, preferred_element_type=jnp.float32)]
    unnamed x111 -> x0, local copies, waits for them, and re-layouts: 29.7 us -> none
    another operation x9 -> x0, local copies, waits for them, and re-layouts: 17.3 us -> none
  transfers between devices with their start and end apart: 23 -> 0, of which waited for: 18 -> 0; matrix products, arithmetic and copies ran while one was open for 14% -> 0% of each run, Pallas kernels for 0% -> 0%
where the time goes in v1:
time: 165 us
  Pallas kernels  152 us (92%)
  local copies, waits for them, and re-layouts  10.8 us (7%)
  between operations  1.95 us (1%)
    pallas_call x1, Pallas kernels, fused(): pl.pallas_call(functools.partial(layer_kernel, names), name='layer', out_...  149 us

profile of v1, /device:TPU:0, one launch (start us, length us, event | category | flops | bytes accessed | tf_op | source)
XLA Modules:
  0.0 164.6 jit_solution(11646754156904945729)
XLA Ops:
  1.9 1.3 reshape.59.refs_5_
  3.2 1.3 reshape.60.refs_6_
  4.5 1.3 reshape.61.refs_10_
  5.7 1.3 reshape.62.refs_11_
  7.0 1.3 reshape.63.refs_12_
  8.3 1.3 reshape.65.refs_16_
  9.5 1.3 reshape.64.refs_14_
  10.9 149.0 %layer.1 = (bf16[256,768]{1,0:T(8,128)(2,1)}, bf16[256,768]{1,0:T(8,128)(2,1)}, f32[28,768]{1,0:T(8,128)}, f32[2,48,576]{2,1,0:T(8,128)}, f32[2,48,192]{2,1,0:T(...) custom-call(bf16[256,768]{1,0:T(8,128)(2,1)} %bitcast.2, s32[1]{0:T(128)S(6)} %copy.33.refs_1_, s32[1]{0:T(128)S(6)} %copy.34.refs_2_, ...), custom_call_target="tpu_custom_call" | custom-call | tf_op jit(solution)/shard_map/layer/pallas_call | solution.py:733
  159.9 2.8 %outputs.1 = (bf16[1,256,768]{2,1,0:T(8,128)(2,1)}, bf16[1,256,768]{2,1,0:T(8,128)(2,1)}, f32[16,768]{1,0:T(8,128)}, f32[768]{0:T(1024)}, f32[768]{0:T(1024)}, /...) custom-call(bf16[256,768]{1,0:T(8,128)(2,1)} %get-tuple-element.22.r, ...), custom_call_target="tpu_custom_call" | custom-call | tf_op jit(solution)/shard_map/outputs/pallas_call | solution.py:745
  162.7 1.9 %copy.32 = f32[384,192]{0,1:T(8,128)} copy(f32[384,192]{1,0:T(8,128)} %get-tuple-element.42) | data formatting | bytes 589824 | tf_op jit(solution)/shard_map/outputs/pallas_call | solution.py:745

commit v2 on v1

--- a/solution.py
+++ b/solution.py
@@ -19,6 +19,7 @@
 
 
 VMEM_LIMIT = 64 << 20
+GROUP = 6
 
 
 BF = jnp.bfloat16
@@ -57,9 +58,10 @@
         self.along_y = (flipped(self.d, 4), self.z)
         self.z_near = (self.d, flipped(self.z, 1))
         self.z_far = (self.d, flipped(self.z, 2))
-
-    def around(self, k):
-        return (self.d, lax.rem(self.z + k, 4))
+        self.z_mirror = (self.d, 3 - self.z)
+
+    def along_z(self, k):
+        return (self.d, self.z + k)
 
 
 def send(src, dst, sems, index, to):
@@ -78,52 +80,82 @@
     def __init__(self, place, g, rc, r1, r2, rz1, rz2, core_sems, sems, parts):
         self.p, self.g, self.rc, self.r1, self.r2 = place, g, rc, r1, r2
         self.rz1, self.rz2, self.core_sems, self.sems, self.parts = rz1, rz2, core_sems, sems, parts
-
-    def core_copy(self, part):
+        self.count = 4 if parts else 1
+
+    def core_copy(self, k):
+        p = self.p
+        kh, kl = k // 2, lax.rem(k, 2)
+        if self.parts == "yx":
+            src, dst = self.g.at[:, kh, kl, 1 - p.c], self.rc.at[:, kh, kl]
+        elif self.parts == "z":
+            src, dst = self.g.at[:, :, :, 1 - p.c, kh, kl], self.rc.at[:, :, :, kh, kl]
+        else:
+            src, dst = self.g.at[:, :, :, 1 - p.c], self.rc
+        return send(src, dst, self.core_sems, k, p.core)
+
+    def core_start(self, k):
+        self.core_copy(k).start()
+
+    def core_sum(self, k):
+        p, g, rc = self.p, self.g, self.rc
+        kh, kl = k // 2, lax.rem(k, 2)
+        self.core_copy(k).wait()
+        if self.parts == "yx":
+            for h in range(2):
+                g[h, kh, kl, p.c] = g[h, kh, kl, p.c] + rc[h, kh, kl]
+            return
+
+        def add(i, _):
+            h, y, x = i // 4, lax.rem(i // 2, 2), lax.rem(i, 2)
+            if self.parts == "z":
+                g[h, y, x, p.c, kh, kl] = g[h, y, x, p.c, kh, kl] + rc[h, y, x, kh, kl]
+            else:
+                g[h, y, x, p.c] = g[h, y, x, p.c] + rc[h, y, x]
+            return 0
+
+        lax.fori_loop(0, 8, add, 0)
+
+    def first_x(self, k):
+        p, g, r1 = self.p, self.g, self.r1
+        kh, kl = k // 2, lax.rem(k, 2)
+        if self.parts == "yx":
+            return send(g.at[0, kh, 1 - p.x, p.c], r1.at[0, kh], self.sems, kh, p.along_x)
+        if self.parts == "z":
+            return send(
+                g.at[0, :, 1 - p.x, p.c, kh, kl], r1.at[0, :, kh, kl], self.sems, k, p.along_x
+            )
+        return send(g.at[0, :, 1 - p.x, p.c], r1.at[0], self.sems, 0, p.along_x)
+
+    def first_y(self, k):
+        p, g, r1 = self.p, self.g, self.r1
+        kh, kl = k // 2, lax.rem(k, 2)
+        if self.parts == "yx":
+            return send(g.at[1, 1 - p.y, kl, p.c], r1.at[1, kl], self.sems, 4 + kl, p.along_y)
+        if self.parts == "z":
+            return send(
+                g.at[1, 1 - p.y, :, p.c, kh, kl], r1.at[1, :, kh, kl], self.sems, 4 + k, p.along_y
+            )
+        return send(g.at[1, 1 - p.y, :, p.c], r1.at[1], self.sems, 4, p.along_y)
+
+    def first_start(self, k):
         p = self.p
         if self.parts == "yx":
-            ky, kx = part // 2, lax.rem(part, 2)
-            src = self.g.at[:, ky, kx, 1 - p.c]
-            dst = self.rc.at[:, ky, kx]
-        elif self.parts == "z":
-            kh, kl = part // 2, lax.rem(part, 2)
-            src = self.g.at[:, :, :, 1 - p.c, kh, kl]
-            dst = self.rc.at[:, :, :, kh, kl]
+            pl.when(lax.rem(k, 2) != p.x)(lambda: self.first_x(k).start())
+            pl.when(k // 2 != p.y)(lambda: self.first_y(k).start())
         else:
-            src = self.g.at[:, :, :, 1 - p.c]
-            dst = self.rc
-        return send(src, dst, self.core_sems, part, p.core)
-
-    def core_start(self, part):
-        self.core_copy(part).start()
-
-    def core_sum(self):
-        p = self.p
-        for part in range(4 if self.parts else 1):
-            self.core_copy(part).wait()
-
-        def add(i, _):
-            h, ky, kx = i // 4, lax.rem(i // 2, 2), lax.rem(i, 2)
-            self.g[h, ky, kx, p.c] = self.g[h, ky, kx, p.c] + self.rc[h, ky, kx]
-            return 0
-
-        lax.fori_loop(0, 8, add, 0)
-
-    def first_copies(self):
-        p, g = self.p, self.g
-        return (
-            send(g.at[0, :, 1 - p.x, p.c], self.r1.at[0], self.sems, 0, p.along_x),
-            send(g.at[1, 1 - p.y, :, p.c], self.r1.at[1], self.sems, 1, p.along_y),
-        )
-
-    def first_start(self):
-        for copy in self.first_copies():
-            copy.start()
+            self.first_x(k).start()
+            self.first_y(k).start()
 
     def first_sum(self):
         p, g = self.p, self.g
-        for copy in self.first_copies():
-            copy.wait()
+        if self.parts == "yx":
+            for i in range(2):
+                self.first_x(2 * i).wait()
+                self.first_y(i).wait()
+        else:
+            for k in range(self.count):
+                self.first_x(k).wait()
+                self.first_y(k).wait()
         for i in range(2):
             g[0, i, p.x, p.c] = g[0, i, p.x, p.c] + self.r1[0, i]
             g[1, p.y, i, p.c] = g[1, p.y, i, p.c] + self.r1[1, i]
@@ -131,8 +163,8 @@
     def second_copies(self):
         p, g = self.p, self.g
         return (
-            send(g.at[0, 1 - p.y, p.x, p.c], self.r2.at[0], self.sems, 2, p.along_y),
-            send(g.at[1, p.y, 1 - p.x, p.c], self.r2.at[1], self.sems, 3, p.along_x),
+            send(g.at[0, 1 - p.y, p.x, p.c], self.r2.at[0], self.sems, 8, p.along_y),
+            send(g.at[1, p.y, 1 - p.x, p.c], self.r2.at[1], self.sems, 9, p.along_x),
         )
 
     def second_start(self):
@@ -148,7 +180,7 @@
 
     def third_copy(self):
         p, g = self.p, self.g
-        return send(g.at[:, p.y, p.x, p.c, :, 1 - p.zl], self.rz1, self.sems, 4, p.z_near)
+        return send(g.at[:, p.y, p.x, p.c, :, 1 - p.zl], self.rz1, self.sems, 10, p.z_near)
 
     def third_start(self):
         self.third_copy().start()
@@ -163,7 +195,7 @@
 
     def fourth_copy(self):
         p, g = self.p, self.g
-        return send(g.at[:, p.y, p.x, p.c, 1 - p.zh, p.zl], self.rz2, self.sems, 5, p.z_far)
+        return send(g.at[:, p.y, p.x, p.c, 1 - p.zh, p.zl], self.rz2, self.sems, 11, p.z_far)
 
     def fourth_start(self):
         self.fourth_copy().start()
@@ -198,28 +230,39 @@
     r = types.SimpleNamespace(**dict(zip(names, refs)))
     p = Place()
     T, D = r.tokens.shape
-    U = HEADS // 4
-    HF = U * HEAD
 
     barrier = pltpu.get_barrier_semaphore()
-    partners = [p.core, p.along_x, p.along_y] + [p.around(k) for k in (1, 2, 3)]
+    partners = (p.core, p.along_x, p.along_y, p.z_near, p.z_far, p.z_mirror)
     for partner in partners:
         pl.semaphore_signal(barrier, inc=1, device_id=partner, device_id_type=MESH)
 
     pool = r.pool
-    load_sems = r.load_sems
 
     def load(src, dst, index):
-        copy = pltpu.make_async_copy(src, dst, load_sems.at[index])
-        copy.start()
-        return copy
+        return pltpu.make_async_copy(src, dst, r.load_sems.at[index])
+
+    def slot_of(k):
+        return jnp.where(k == 2, 1, 4 + 2 * lax.rem(k, 3))
+
+    def up_load(k):
+        src = r.up_weight.at[:, pl.ds(pl.multiple_of(k * D, D), D)]
+        return load(src, pool.at[slot_of(k)], 6 + k)
+
+    def down_load(k):
+        src = r.down_weight.at[pl.ds(pl.multiple_of(k * D, D), D), :]
+        return load(src, pool.at[slot_of(k) + 1], 10 + k)
 
     tokens_load = load(r.tokens, r.tok, 0)
+    tokens_load.start()
     qkv_loads = [
         load(r.qkv_weight.at[:, pl.ds(i * D, D)], pool.at[1 + i], 1 + i) for i in range(3)
     ]
+    for i in (1, 2, 0):
+        qkv_loads[i].start()
     cot_load = load(r.cotangent, r.cot, 4)
     out_load = load(r.out_weight, pool.at[0], 5)
+    for copy in (cot_load, out_load, up_load(0), down_load(0), up_load(1), down_load(1)):
+        copy.start()
 
     gid = r.group_ids[0]
     length = r.lengths[0]
@@ -228,116 +271,104 @@
     table_row = jnp.sum(jnp.where(group_rows == gid, table, 0.0), axis=0, keepdims=True)
     tokens_load.wait()
     start = r.tok[...].astype(F32) + table_row
-    r.start[...] = start
     mean, inverse = norm_stats(start)
-    norm_one = ((start - mean) * inverse * r.first_gain[...] + r.first_shift[...]).astype(BF)
-    r.norm_oneT[...] = norm_one.T
-    mix = r.mix
-    qv_bias = r.qv_bias
-    for i in range(3):
-        qkv_loads[i].wait()
-        rows = dot(norm_one, pool[1 + i])
-        if i != 1:
-            rows = rows + qv_bias[pl.ds(i // 2, 1), :]
-        mix[i] = rows.astype(BF).T
-    up_loads = [
-        load(r.up_weight.at[:, pl.ds(i * D, D)], pool.at[1 + i], 6 + i) for i in range(4)
-    ]
-    down_loads = [
-        load(r.down_weight.at[pl.ds(i * D, D), :], pool.at[5 + i], 10 + i) for i in range(4)
-    ]
+    nx, nxT = r.nx, r.nxT
+    nx[0] = ((start - mean) * inverse * row_of(r.first_gain) + row_of(r.first_shift)).astype(BF)
 
     pl.semaphore_wait(barrier, len(partners))
 
-    qkv = r.qkv
-
-    def unit_rows(s, u):
-        return pl.ds(pl.multiple_of((s * U + u) * HEAD, HEAD), HEAD)
-
-    def qkv_copy(k, u):
-        to = p.around(k)
-        return send(
-            mix.at[:, unit_rows(to[1], u), :], qkv.at[u, p.z], r.qkv_sems, u * 3 + k - 1, to
-        )
-
-    for u in range(U):
-        for k in (1, 2, 3):
-            qkv_copy(k, u).start()
-    own_qkv = []
-    for u in range(U):
-        copy = pltpu.make_async_copy(
-            mix.at[:, unit_rows(p.z, u), :], qkv.at[u, p.z], r.own_sems.at[u]
-        )
-        copy.start()
-        own_qkv.append(copy)
-
-    cot_load.wait()
-    cot = r.cot[...]
-    r.cotT[...] = cot.T
-
+    def nx_copy(s):
+        return send(nx.at[s], nx.at[s + 1], r.nx_sems, s, p.along_z(1))
+
+    def nx_wait(s):
+        return send(nx.at[s - 1], nx.at[s], r.nx_sems, s - 1, p.along_z(-1)).wait_recv()
+
+    kv, qT, outT, top, mass = r.kv, r.qT, r.outT, r.top, r.mass
     key_iota = lax.broadcasted_iota(jnp.int32, (T, T), 0)
     query_iota = lax.broadcasted_iota(jnp.int32, (T, T), 1)
     scale2 = HEAD**-0.5 * LOG2E
 
-    def masked(u, i, j):
-        scores = dot_tn(qkv[u, j, 1], qkv[u, i, 0]) * scale2
-        allowed = key_iota < length - j * T
-        if i == j:
+    def head_rows(h):
+        return pl.ds(pl.multiple_of(h * HEAD, HEAD), HEAD)
+
+    def masked(s, rows):
+        scores = dot_tn(kv[s, 0, rows], qT[rows]) * scale2
+        allowed = key_iota < length - (p.z - s) * T
+        if s == 0:
             allowed = allowed & (key_iota <= query_iota)
         return jnp.where(allowed, scores, NEG_LARGE)
 
-    attT, outT, out_low, lse = r.attT, r.outT, r.out_low, r.lse
-
-    def att_copy(k, u):
-        to = p.around(k)
-        return send(
-            out_low.at[u, to[1]],
-            attT.at[unit_rows(p.z, u), :],
-            r.att_sems,
-            u * 3 + k - 1,
-            to,
-        )
-
-    own_att = []
-    for u in range(U):
-        own_qkv[u].wait()
-        for k in (1, 2, 3):
-            qkv_copy(k, u).wait()
-        for i in range(4):
-            blocks = [masked(u, i, j) for j in range(i + 1)]
-            top = functools.reduce(
-                jnp.maximum, [jnp.max(b, axis=0, keepdims=True) for b in blocks]
-            )
-            weights = [jnp.exp2(b - top) for b in blocks]
-            total = sum(jnp.sum(w, axis=0, keepdims=True) for w in weights)
-            acc = sum(dot(qkv[u, j, 2], weights[j].astype(BF)) for j in range(i + 1))
-            value = acc * (1.0 / total)
-            outT[u, i] = value
-            out_low[u, i] = value.astype(BF)
-            lse[u, i] = top + jnp.log2(total)
-        for k in (1, 2, 3):
-            att_copy(k, u).start()
-        copy = pltpu.make_async_copy(
-            out_low.at[u, p.z], attT.at[unit_rows(p.z, u), :], r.own_sems.at[U + u]
-        )
-        copy.start()
-        own_att.append(copy)
-    for u in range(U):
-        own_att[u].wait()
-        for k in (1, 2, 3):
-            att_copy(k, u).wait()
+    def attend(s):
+        def some_heads(g, _):
+            heads = [g * GROUP + i for i in range(GROUP)]
+            places = [head_rows(h) for h in heads]
+            scores = [masked(s, rows) for rows in places]
+            highest = [jnp.max(v, axis=0, keepdims=True) for v in scores]
+            if s > 0:
+                highest = [jnp.maximum(v, top[h]) for v, h in zip(highest, heads)]
+                fade = [jnp.exp2(top[h] - v) for v, h in zip(highest, heads)]
+            weights = [jnp.exp2(v - m) for v, m in zip(scores, highest)]
+            total = [column_sum(v) for v in weights]
+            value = [dot(kv[s, 1, rows], v.astype(BF)) for v, rows in zip(weights, places)]
+            for i, (h, rows) in enumerate(zip(heads, places)):
+                if s > 0:
+                    total[i] = total[i] + mass[h] * fade[i]
+                    value[i] = value[i] + outT[rows] * fade[i]
+                top[h] = highest[i]
+                mass[h] = total[i]
+                outT[rows] = value[i]
+            return 0
+
+        lax.fori_loop(0, HEADS // GROUP, some_heads, 0)
+
+    def forward_step(s):
+        if s > 0:
+            nx_wait(s)
+        if s < 3:
+            pl.when(p.z < 3)(lambda: nx_copy(s).start())
+        block = nx[s]
+        nxT[:, s * T : (s + 1) * T] = block.T
+        if s == 0:
+            qkv_loads[1].wait()
+        kv[s, 0] = dot(block, pool[2]).astype(BF).T
+        if s == 0:
+            qkv_loads[2].wait()
+        kv[s, 1] = (dot(block, pool[3]) + r.qv_bias[1:2]).astype(BF).T
+        if s == 0:
+            qkv_loads[0].wait()
+            qT[...] = (dot(block, pool[1]) + r.qv_bias[0:1]).astype(BF).T
+        attend(s)
+
+    forward_step(0)
+    cot_load.wait()
+    r.cotT[...] = r.cot[...].T
+    for k in range(4):
+        r.up_rows[k : k + 1] = r.up_bias[k * D : (k + 1) * D].reshape(1, D)
+    for s in (1, 2, 3):
+        pl.when(p.z >= s)(functools.partial(forward_step, s))
+    up_load(2).start()
+    down_load(2).start()
+
+    def finish(h, _):
+        rows = head_rows(h)
+        value = outT[rows] * (1.0 / mass[h])
+        outT[rows] = value
+        r.attT[rows] = value.astype(BF)
+        top[h] = top[h] + jnp.log2(mass[h])
+        return 0
+
+    lax.fori_loop(0, HEADS, finish, 0, unroll=True)
+    attT = r.attT
 
     out_load.wait()
-    after = start_of(r) + dot(attT[...].T, pool[0]) + r.out_bias[...]
+    after = r.tok[...].astype(F32) + table_row + dot(attT[...].T, pool[0]) + row_of(r.out_bias)
     r.after[...] = after
     mean, inverse = norm_stats(after)
-    norm_two = ((after - mean) * inverse * r.second_gain[...] + r.second_shift[...]).astype(BF)
+    norm_two = ((after - mean) * inverse * row_of(r.second_gain) + row_of(r.second_shift)).astype(BF)
     r.norm_two[...] = norm_two
     r.norm_twoT[...] = norm_two.T
-    r.total[...] = after + r.down_bias[...]
+    r.total[...] = after + row_of(r.down_bias)
     r.t[...] = jnp.zeros((T, D), F32)
-    for copy in up_loads + down_loads:
-        copy.wait()
 
     g_down, g_up, g_out, g_qkv = r.g_down, r.g_up, r.g_out, r.g_qkv
 
@@ -362,11 +393,19 @@
     small = r.small
     gelu_c = math.sqrt(2.0 / math.pi)
 
+    def pass_on(k):
+        down.core_sum(k)
+        down.first_start(k)
+        up.core_sum(k)
+        up.first_start(k)
+
     def chunk(k, _):
         kh, kl = k // 2, lax.rem(k, 2)
-        weight = pool[1 + k]
-        weight_down = pool[5 + k]
-        hidden = dot(r.norm_two[...], weight) + r.up_bias[pl.ds(k, 1), :]
+        up_load(k).wait()
+        down_load(k).wait()
+        weight = pool[slot_of(k)]
+        weight_down = pool[slot_of(k) + 1]
+        hidden = dot(r.norm_two[...], weight) + r.up_rows[pl.ds(k, 1), :]
         act_grad = dot_nt(r.cot[...], weight_down)
         square = hidden * hidden
         th = jnp.tanh(gelu_c * hidden * (1.0 + 0.044715 * square))
@@ -376,8 +415,6 @@
         grad = act_grad * slope
         small[pl.ds(24 + k, 1), :] = column_sum(grad)
         low = grad.astype(BF)
-        r.total[...] += dot(act, weight_down)
-        r.t[...] += dot_nt(low, weight)
         piece = D // 2
         for cc in range(2):
             rows = dot(r.cotT[...], act[:, cc * piece : (cc + 1) * piece]).astype(BF)
@@ -394,37 +431,39 @@
                 at = d * part + h * (part // 2)
                 g_up[h, d // 4, (d // 2) % 2, d % 2, kh, kl] = rows[at : at + part // 2]
         up.core_start(k)
+        r.total[...] += dot(act, weight_down)
+        r.t[...] += dot_nt(low, weight)
+
+        def last_load():
+            up_load(3).start()
+            down_load(3).start()
+
+        pl.when(k == 0)(last_load)
+        pl.when(k > 0)(lambda: pass_on(k - 1))
         return 0
 
     lax.fori_loop(0, 4, chunk, 0)
+    pass_on(3)
 
     qkv_loads = [
         load(r.qkv_weight.at[:, pl.ds(i * D, D)], pool.at[1 + i], 14 + i) for i in range(3)
     ]
-
-    r.result[...] = r.total[...].astype(BF)
+    for copy in qkv_loads:
+        copy.start()
+
+    nx[3] = r.total[...].astype(BF)
+    result_store = pltpu.make_async_copy(nx.at[3], r.result, r.load_sems.at[17])
+    result_store.start()
     cot = r.cot[...].astype(F32)
     after = r.after[...]
     mean, inverse = norm_stats(after)
     n = (after - mean) * inverse
     t = r.t[...]
-    after_grad = cot + norm_back(t, r.second_gain[...], n, inverse)
-    r.after_grad[...] = after_grad
+    after_grad = cot + norm_back(t, row_of(r.second_gain), n, inverse)
+    r.after[...] = after_grad
     after_low = after_grad.astype(BF)
-    doT, dor = r.doT, r.dor
+    doT = r.doT
     doT[...] = dot_nt(pool[0], after_low).astype(BF)
-
-    def do_copy(k):
-        to = p.around(k)
-        rows = pl.ds(pl.multiple_of(to[1] * HF, HF), HF)
-        return send(doT.at[rows, :], dor.at[p.z], r.do_sems, k - 1, to)
-
-    for k in (1, 2, 3):
-        do_copy(k).start()
-    own_do = pltpu.make_async_copy(
-        doT.at[pl.ds(pl.multiple_of(p.z * HF, HF), HF), :], dor.at[p.z], r.own_sems.at[2 * U]
-    )
-    own_do.start()
     small[pl.ds(20, 1), :] = column_sum(after_grad)
     small[pl.ds(21, 1), :] = column_sum(t * n)
     small[pl.ds(22, 1), :] = column_sum(t)
@@ -439,107 +478,131 @@
                 g_out[h, d // 4, (d // 2) % 2, d % 2, z // 2, z % 2] = rows[at : at + part // 2]
     out.core_start(0)
 
-    down.core_sum()
-    down.first_start()
-    up.core_sum()
-    up.first_start()
-    out.core_sum()
-    out.first_start()
-
-    own_do.wait()
-    for k in (1, 2, 3):
-        do_copy(k).wait()
-    mgT = r.mgT
-
-    def back_copy(k, u):
-        to = p.around(k)
-        return send(
-            mix.at[:, unit_rows(to[1], u), :],
-            mgT.at[:, unit_rows(p.z, u), :],
-            r.back_sems,
-            u * 3 + k - 1,
-            to,
-        )
-
-    own_back = []
-    for u in range(U):
-        key_grads = [jnp.zeros((HEAD, T), F32) for _ in range(4)]
-        value_grads = [jnp.zeros((HEAD, T), F32) for _ in range(4)]
-        for i in range(4):
-            do_i = dor[i, u * HEAD : (u + 1) * HEAD]
-            delta = column_sum(do_i.astype(F32) * outT[u, i])
-            lse_i = lse[u, i]
-            query_grad = jnp.zeros((HEAD, T), F32)
-            for j in range(i + 1):
-                probs = jnp.exp2(masked(u, i, j) - lse_i)
-                prob_grad = dot_tn(qkv[u, j, 2], do_i)
-                score_grad = (probs * (prob_grad - delta)).astype(BF)
-                query_grad += dot(qkv[u, j, 1], score_grad)
-                key_grads[j] += dot_nt(qkv[u, i, 0], score_grad)
-                value_grads[j] += dot_nt(do_i, probs.astype(BF))
-            mix[0, (i * U + u) * HEAD : (i * U + u + 1) * HEAD] = (query_grad * HEAD**-0.5).astype(BF)
-        for j in range(4):
-            rows = slice((j * U + u) * HEAD, (j * U + u + 1) * HEAD)
-            mix[1, rows] = (key_grads[j] * HEAD**-0.5).astype(BF)
-            mix[2, rows] = value_grads[j].astype(BF)
-        for k in (1, 2, 3):
-            back_copy(k, u).start()
-        copy = pltpu.make_async_copy(
-            mix.at[:, unit_rows(p.z, u), :],
-            mgT.at[:, unit_rows(p.z, u), :],
-            r.own_sems.at[2 * U + 1 + u],
-        )
-        copy.start()
-        own_back.append(copy)
-        if u == 1:
-            down.first_sum()
-            down.second_start()
-    up.first_sum()
-    up.second_start()
-    out.first_sum()
-    out.second_start()
-    down.second_sum()
-    down.third_start()
-    up.second_sum()
-    up.third_start()
-    out.second_sum()
-    out.third_start()
-
-    for u in range(U):
-        own_back[u].wait()
-        for k in (1, 2, 3):
-            back_copy(k, u).wait()
-
+    delta = r.delta
+    for h in range(HEADS):
+        rows = slice(h * HEAD, (h + 1) * HEAD)
+        delta[h] = column_sum(doT[rows].astype(F32) * outT[rows])
+    outT[...] = jnp.zeros((D, T), F32)
+    mg = r.mg
+
+    def attend_back(s):
+        lanes = slice(s * T, (s + 1) * T)
+
+        def some_heads(g, _):
+            heads = [g * GROUP + i for i in range(GROUP)]
+            places = [head_rows(h) for h in heads]
+            scores = [masked(s, rows) for rows in places]
+            prob_grad = [dot_tn(kv[s, 1, rows], doT[rows]) for rows in places]
+            probs = [jnp.exp2(v - top[h]) for v, h in zip(scores, heads)]
+            score_grad = [
+                (v * (w - delta[h])).astype(BF) for v, w, h in zip(probs, prob_grad, heads)
+            ]
+            probs = [v.astype(BF) for v in probs]
+            query_add = [dot(kv[s, 0, rows], v) for v, rows in zip(score_grad, places)]
+            key_add = [dot_nt(qT[rows], v) for v, rows in zip(score_grad, places)]
+            value_add = [dot_nt(doT[rows], v) for v, rows in zip(probs, places)]
+            for i, rows in enumerate(places):
+                outT[rows] = outT[rows] + query_add[i]
+                mg[0, rows, lanes] = (key_add[i] * HEAD**-0.5).astype(BF)
+                mg[1, rows, lanes] = value_add[i].astype(BF)
+            return 0
+
+        lax.fori_loop(0, HEADS // GROUP, some_heads, 0)
+
+    def t1_of(s):
+        lanes = slice(s * T, (s + 1) * T)
+        return dot(pool[2], mg[0, :, lanes]) + dot(pool[3], mg[1, :, lanes])
+
+    def t1_copy(s):
+        return send(kv.at[s, 0], r.t1_in.at[s - 1], r.t1_sems, s - 1, p.along_z(-1))
+
+    def t1_wait(s):
+        send(kv.at[s + 1, 0], r.t1_in.at[s], r.t1_sems, s, p.along_z(1)).wait_recv()
+
+    def back_step(s):
+        attend_back(s)
+        kv[s, 0] = t1_of(s).astype(BF)
+        pl.when(p.z == 3)(lambda: t1_copy(s).start())
+
+    def no_step(s):
+        lanes = slice(s * T, (s + 1) * T)
+        nxT[:, lanes] = jnp.zeros((D, T), BF)
+        for i in range(2):
+            mg[i, :, lanes] = jnp.zeros((D, T), BF)
+
+    for copy in qkv_loads:
+        copy.wait()
+    for s in (3, 2, 1):
+        pl.when(p.z >= s)(functools.partial(back_step, s))
+        pl.when(p.z < s)(functools.partial(no_step, s))
+        if s == 3:
+            out.core_sum(0)
+            out.first_start(0)
+    attend_back(0)
+
+    query_grad = outT[...] * HEAD**-0.5
+    query_low = query_grad.astype(BF)
     share = 3 * D // 4
     part = D // 8
     for z in range(4):
-        a, b = z * share // D, (z + 1) * share // D
-        cut = (z + 1) * share - b * D
-        pieces = [mgT[a, z * share - a * D : (D if b > a else cut)]]
-        if b > a and cut > 0:
-            pieces.append(mgT[b, 0:cut])
-        pieces = pieces[0] if len(pieces) == 1 else jnp.concatenate(pieces, axis=0)
-        rows = dot_nt(r.norm_oneT[...], pieces).astype(BF)
+        columns = []
+        for i in range(3):
+            low_at, high_at = max(z * share, i * D) - i * D, min((z + 1) * share, (i + 1) * D) - i * D
+            if low_at >= high_at:
+                continue
+            if i == 0:
+                columns.append(dot_nt(nxT[:, 0:T], query_low[low_at:high_at]))
+            else:
+                columns.append(dot_nt(nxT[...], mg[i - 1, low_at:high_at]))
+        rows = (columns[0] if len(columns) == 1 else jnp.concatenate(columns, axis=1)).astype(BF)
         for d in range(8):
             for h in range(2):
                 at = d * part + h * (part // 2)
                 g_qkv[h, d // 4, (d // 2) % 2, d % 2, z // 2, z % 2] = rows[at : at + part // 2]
     proj.core_start(0)
-    for copy in qkv_loads:
-        copy.wait()
-    t1 = dot(pool[1], mgT[0]) + dot(pool[2], mgT[1]) + dot(pool[3], mgT[2])
-    t1 = t1.T
-    start = r.start[...]
+    t1 = t1_of(0) + dot(pool[1], query_low)
+    r.outT[...] = t1
+    ones = jnp.ones((8, 4 * T), BF)
+    small[pl.ds(18, 1), :] = dot_nt(ones[:, 0:T], query_low)[0:1]
+    small[pl.ds(19, 1), :] = dot_nt(ones, mg[1])[0:1]
+
+    down.first_sum()
+    down.second_start()
+    proj.core_sum(0)
+    proj.first_start(0)
+
+    def t1_pass(s):
+        t1_wait(s)
+        kv[s, 0] = kv[s, 0] + r.t1_in[s]
+        t1_copy(s).start()
+
+    pl.when(p.z == 2)(lambda: t1_pass(2))
+    up.first_sum()
+    up.second_start()
+    out.first_sum()
+    out.second_start()
+    pl.when((p.z >= 1) & (p.z < 3))(lambda: t1_pass(1))
+    down.second_sum()
+    down.third_start()
+    up.second_sum()
+    up.third_start()
+
+    def t1_last():
+        t1_wait(0)
+        outT[...] = outT[...] + r.t1_in[0].astype(F32)
+
+    pl.when(p.z < 3)(t1_last)
+    t1 = outT[...].T
+    start = r.tok[...].astype(F32) + table_row
     mean, inverse = norm_stats(start)
     n = (start - mean) * inverse
-    start_grad = r.after_grad[...] + norm_back(t1, r.first_gain[...], n, inverse)
-    r.grad_tokens[...] = start_grad.astype(BF)
-    ones = jnp.ones((8, T), BF)
+    start_grad = r.after[...] + norm_back(t1, row_of(r.first_gain), n, inverse)
+    r.norm_two[...] = start_grad.astype(BF)
+    tokens_store = pltpu.make_async_copy(r.norm_two, r.grad_tokens, r.load_sems.at[18])
+    tokens_store.start()
     small[pl.ds(0, 16), :] = jnp.where(group_rows == gid, column_sum(start_grad), 0.0)
     small[pl.ds(16, 1), :] = column_sum(t1 * n)
     small[pl.ds(17, 1), :] = column_sum(t1)
-    small[pl.ds(18, 1), :] = dot_nt(ones, mgT[0])[0:1]
-    small[pl.ds(19, 1), :] = dot_nt(ones, mgT[2])[0:1]
 
     small_in, small_sems = r.small_in, r.small_sems
     small_to = [p.core, p.along_x, p.along_y, p.z_near, p.z_far]
@@ -552,38 +615,44 @@
         small[...] = small[...] + small_in[step]
 
     small_copy(0).start()
-    proj.core_sum()
-    proj.first_start()
+    out.second_sum()
+    out.third_start()
+    down.third_sum()
+    down.fourth_start()
     small_sum(0)
     small_copy(1).start()
-    down.third_sum()
-    down.fourth_start()
+    proj.first_sum()
+    proj.second_start()
     up.third_sum()
     up.fourth_start()
+    small_sum(1)
+    small_copy(2).start()
     out.third_sum()
     out.fourth_start()
-    small_sum(1)
-    small_copy(2).start()
-    proj.first_sum()
-    proj.second_start()
     small_sum(2)
     small_copy(3).start()
-    down.fourth_sum(r.s_down)
-    up.fourth_sum(r.s_up)
-    out.fourth_sum(r.s_out)
     proj.second_sum()
     proj.third_start()
     small_sum(3)
     small_copy(4).start()
+    down.fourth_sum(r.s_down)
+    up.fourth_sum(r.s_up)
+    out.fourth_sum(r.s_out)
     proj.third_sum()
     proj.fourth_start()
     small_sum(4)
     r.small_out[...] = small[...]
+    for s in (0, 1, 2):
+        pl.when((p.z < 3) & (p.z >= s))(lambda s=s: nx_copy(s).wait_send())
+    for s in (1, 2, 3):
+        pl.when(p.z >= s)(lambda s=s: t1_copy(s).wait_send())
+    result_store.wait()
+    tokens_store.wait()
     proj.fourth_sum(r.s_qkv)
 
 
-def start_of(r):
-    return r.start[...]
+def row_of(ref):
+    return ref[...].reshape(1, ref.shape[0])
 
 
 def outputs_kernel(result, grad_tokens, small, s_qkv, s_out, s_up, s_down, *outs):
@@ -620,12 +689,10 @@
         ref[...] = small[row]
     for k in range(4):
         o_up_bias[pl.ds(k * D, D)] = small[24 + k]
-    for ref, value in ((o_qkv, s_qkv), (o_out, s_out), (o_up, s_up)):
+    for ref, value in ((o_qkv, s_qkv), (o_out, s_out), (o_up, s_up), (o_down, s_down)):
         half = value.shape[1]
         for h in range(2):
             ref[h * half : (h + 1) * half] = value[h]
-    half = s_down.shape[1]
-    o_down[...] = jnp.concatenate([s_down[0], s_down[1]], axis=0).T
 
 
 def fused(
@@ -649,7 +716,6 @@
 ):
     _, T, D = tokens.shape
     F = up_weight.shape[1]
-    U = HEADS // 4
     any_spec = pl.BlockSpec(memory_space=pl.ANY)
     vmem = pl.BlockSpec(memory_space=pltpu.VMEM)
     smem = pl.BlockSpec(memory_space=pltpu.SMEM)
@@ -659,18 +725,18 @@
         lengths=(lengths, smem),
         cotangent=(cotangent.reshape(T, D), any_spec),
         group_table=(group_table, vmem),
-        first_gain=(first_gain.reshape(1, D), vmem),
-        first_shift=(first_shift.reshape(1, D), vmem),
+        first_gain=(first_gain, vmem),
+        first_shift=(first_shift, vmem),
         qkv_weight=(qkv_weight, any_spec),
         qv_bias=(query_value_bias, vmem),
         out_weight=(out_weight, any_spec),
-        out_bias=(out_bias.reshape(1, D), vmem),
-        second_gain=(second_gain.reshape(1, D), vmem),
-        second_shift=(second_shift.reshape(1, D), vmem),
+        out_bias=(out_bias, vmem),
+        second_gain=(second_gain, vmem),
+        second_shift=(second_shift, vmem),
         up_weight=(up_weight, any_spec),
-        up_bias=(up_bias.reshape(4, D), vmem),
+        up_bias=(up_bias, vmem),
         down_weight=(down_weight, any_spec),
-        down_bias=(down_bias.reshape(1, D), vmem),
+        down_bias=(down_bias, vmem),
     )
     shares = dict(
         down=(D // 8, F // 8),
@@ -686,35 +752,33 @@
     outputs.update({"s_" + k: ((2,) + shares[k], F32) for k in ("qkv", "out", "up", "down")})
     dma = pltpu.SemaphoreType.DMA
     scratch = dict(
-        pool=pltpu.VMEM((9, D, D), BF),
+        pool=pltpu.VMEM((8, D, D), BF),
         tok=pltpu.VMEM((T, D), BF),
         cot=pltpu.VMEM((T, D), BF),
         cotT=pltpu.VMEM((D, T), BF),
-        start=pltpu.VMEM((T, D), F32),
-        norm_oneT=pltpu.VMEM((D, T), BF),
-        mix=pltpu.VMEM((3, D, T), BF),
-        qkv=pltpu.VMEM((U, 4, 3, HEAD, T), BF),
-        outT=pltpu.VMEM((U, 4, HEAD, T), F32),
-        out_low=pltpu.VMEM((U, 4, HEAD, T), BF),
-        lse=pltpu.VMEM((U, 4, 1, T), F32),
+        nx=pltpu.VMEM((4, T, D), BF),
+        nxT=pltpu.VMEM((D, 4 * T), BF),
+        qT=pltpu.VMEM((D, T), BF),
+        kv=pltpu.VMEM((4, 2, D, T), BF),
+        outT=pltpu.VMEM((D, T), F32),
+        top=pltpu.VMEM((HEADS, 1, T), F32),
+        mass=pltpu.VMEM((HEADS, 1, T), F32),
+        delta=pltpu.VMEM((HEADS, 1, T), F32),
         attT=pltpu.VMEM((D, T), BF),
         after=pltpu.VMEM((T, D), F32),
         norm_two=pltpu.VMEM((T, D), BF),
         norm_twoT=pltpu.VMEM((D, T), BF),
         total=pltpu.VMEM((T, D), F32),
         t=pltpu.VMEM((T, D), F32),
-        after_grad=pltpu.VMEM((T, D), F32),
         doT=pltpu.VMEM((D, T), BF),
-        dor=pltpu.VMEM((4, U * HEAD, T), BF),
-        mgT=pltpu.VMEM((3, D, T), BF),
+        mg=pltpu.VMEM((2, D, 4 * T), BF),
+        t1_in=pltpu.VMEM((3, D, T), BF),
+        up_rows=pltpu.VMEM((4, D), F32),
         small=pltpu.VMEM((28, D), F32),
         small_in=pltpu.VMEM((5, 28, D), F32),
-        load_sems=dma((17,)),
-        own_sems=dma((3 * U + 1,)),
-        qkv_sems=dma((2, 3 * U)),
-        att_sems=dma((2, 3 * U)),
-        do_sems=dma((2, 3)),
-        back_sems=dma((2, 3 * U)),
+        load_sems=dma((19,)),
+        nx_sems=dma((2, 3)),
+        t1_sems=dma((2, 3)),
         small_sems=dma((2, 5)),
     )
     for name, (rows, columns) in shares.items():
@@ -726,7 +790,7 @@
             "rz1_" + name: pltpu.VMEM((2, 2, rows, columns), BF),
             "rz2_" + name: pltpu.VMEM((2, rows, columns), BF),
             "cs_" + name: dma((2, 4)),
-            "ss_" + name: dma((2, 6)),
+            "ss_" + name: dma((2, 12)),
         }
         scratch.update(extra)
     names = list(inputs) + list(outputs) + list(scratch)
@@ -735,14 +799,14 @@
         name="layer",
         out_shape=[jax.ShapeDtypeStruct(*o) for o in outputs.values()],
         in_specs=[i[1] for i in inputs.values()],
-        out_specs=[vmem] * len(outputs),
+        out_specs=[any_spec] * 2 + [vmem] * (len(outputs) - 2),
         scratch_shapes=list(scratch.values()),
         compiler_params=pltpu.CompilerParams(
             collective_id=0, has_side_effects=True, vmem_limit_bytes=VMEM_LIMIT
         ),
     )(*[i[0] for i in inputs.values()])
     shape = jax.ShapeDtypeStruct
-    return pl.pallas_call(
+    outs = pl.pallas_call(
         outputs_kernel,
         name="outputs",
         out_shape=[
@@ -759,12 +823,13 @@
             shape((D,), F32),
             shape((D // 8, F // 4), F32),
             shape((F,), F32),
-            shape((F // 8, D // 4), F32),
+            shape((D // 4, F // 8), F32),
             shape((D,), F32),
         ],
         in_specs=[vmem] * len(done),
         out_specs=[vmem] * 15,
     )(*done)
+    return (*outs[:13], outs[13].T, outs[14])
 
 
 def shifted(array, axis, by):

time: 165 us -> 137 us (0.83)
  Pallas kernels: 152 us -> 135 us
  local copies, waits for them, and re-layouts: 10.8 us -> 0 us
    pallas_call x1, Pallas kernels: 149 us -> 132 us  [fused(): pl.pallas_call(functools.partial(layer_kernel, names), name='layer', out_...]
    reshape x7 -> x0, local copies, waits for them, and re-layouts: 8.91 us -> none  [the longest x1 1.31 us: fused(): up_bias.reshape(4, D)]
    pallas_call x1 -> x0, local copies, waits for them, and re-layouts: 1.86 us -> none  [fused(): pl.pallas_call(outputs_kernel, name='outputs', out_shape=[shape((1, T, D)...]
where the time goes in v2:
time: 137 us
  Pallas kernels  135 us (99%)
  between operations  2.1 us (2%)
    pallas_call x1, Pallas kernels, fused(): pl.pallas_call(functools.partial(layer_kernel, names), name='layer', out_...  132 us

profile of v2, /device:TPU:0, one launch (start us, length us, event | category | flops | bytes accessed | tf_op | source)
XLA Modules:
  0.0 136.6 jit_solution(6520077306857010065)
XLA Ops:
  1.9 131.8 %layer.1 = (bf16[256,768]{1,0:T(8,128)(2,1)}, bf16[256,768]{1,0:T(8,128)(2,1)}, f32[28,768]{1,0:T(8,128)}, f32[2,48,576]{2,1,0:T(8,128)}, f32[2,48,192]{2,1,0:T(...) custom-call(bf16[256,768]{1,0:T(8,128)(2,1)} %bitcast.3, s32[1]{0:T(128)S(6)} %copy.32.refs_1_, s32[1]{0:T(128)S(6)} %copy.33.refs_2_, ...), custom_call_target="tpu_custom_call" | custom-call | tf_op jit(solution)/shard_map/layer/pallas_call | solution.py:797
  133.8 2.7 %outputs.1 = (bf16[1,256,768]{2,1,0:T(8,128)(2,1)}, bf16[1,256,768]{2,1,0:T(8,128)(2,1)}, f32[16,768]{1,0:T(8,128)}, f32[768]{0:T(1024)}, f32[768]{0:T(1024)}, /...) custom-call(bf16[256,768]{1,0:T(8,128)(2,1)} %get-tuple-element.37.r, ...), custom_call_target="tpu_custom_call" | custom-call | tf_op jit(solution)/shard_map/outputs/pallas_call | solution.py:809

commit v3 on v2

--- a/solution.py
+++ b/solution.py
@@ -59,6 +59,7 @@
         self.z_near = (self.d, flipped(self.z, 1))
         self.z_far = (self.d, flipped(self.z, 2))
         self.z_mirror = (self.d, 3 - self.z)
+        self.diagonal = (flipped(flipped(self.d, 2), 4), self.z)
 
     def along_z(self, k):
         return (self.d, self.z + k)
@@ -77,10 +78,14 @@
 
 
 class ReduceScatter:
-    def __init__(self, place, g, rc, r1, r2, rz1, rz2, core_sems, sems, parts):
+    def __init__(
+        self, place, g, rc, r1, r2, rz1, rz2, core_sems, sems, parts, out, zb=None, columns=None
+    ):
         self.p, self.g, self.rc, self.r1, self.r2 = place, g, rc, r1, r2
         self.rz1, self.rz2, self.core_sems, self.sems, self.parts = rz1, rz2, core_sems, sems, parts
         self.count = 4 if parts else 1
+        self.out, self.columns = out, columns
+        self.zb = g.at[:, place.y, place.x, place.c] if zb is None else zb
 
     def core_copy(self, k):
         p = self.p
@@ -176,36 +181,95 @@
         for copy in self.second_copies():
             copy.wait()
         for h in range(2):
-            g[h, p.y, p.x, p.c] = g[h, p.y, p.x, p.c] + self.r2[h]
+            total = g[h, p.y, p.x, p.c] + self.r2[h]
+            if self.columns is None:
+                g[h, p.y, p.x, p.c] = total
+            else:
+                for z, (first, last) in enumerate(self.columns):
+                    self.zb[h, z // 2, z % 2] = total[:, first:last]
 
     def third_copy(self):
-        p, g = self.p, self.g
-        return send(g.at[:, p.y, p.x, p.c, :, 1 - p.zl], self.rz1, self.sems, 10, p.z_near)
+        p = self.p
+        return send(self.zb.at[:, :, 1 - p.zl], self.rz1, self.sems, 10, p.z_near)
 
     def third_start(self):
         self.third_copy().start()
 
     def third_sum(self):
-        p, g = self.p, self.g
+        p, zb = self.p, self.zb
         self.third_copy().wait()
         for h in range(2):
             for i in range(2):
-                mine = (h, p.y, p.x, p.c, i, p.zl)
-                g[mine] = g[mine] + self.rz1[h, i]
+                zb[h, i, p.zl] = zb[h, i, p.zl] + self.rz1[h, i]
 
     def fourth_copy(self):
-        p, g = self.p, self.g
-        return send(g.at[:, p.y, p.x, p.c, 1 - p.zh, p.zl], self.rz2, self.sems, 11, p.z_far)
+        p = self.p
+        return send(self.zb.at[:, 1 - p.zh, p.zl], self.rz2, self.sems, 11, p.z_far)
 
     def fourth_start(self):
         self.fourth_copy().start()
 
-    def fourth_sum(self, out):
-        p, g = self.p, self.g
+    def fourth_sum(self):
+        p, zb = self.p, self.zb
         self.fourth_copy().wait()
         for h in range(2):
-            mine = (h, p.y, p.x, p.c, p.zh, p.zl)
-            out[h] = g[mine].astype(F32) + self.rz2[h].astype(F32)
+            self.out[h] = zb[h, p.zh, p.zl].astype(F32) + self.rz2[h].astype(F32)
+
+    def advance(self, step):
+        if step == 0:
+            self.core_sum(0)
+            self.first_start(0)
+        elif step == 1:
+            self.first_sum()
+            self.second_start()
+        elif step == 2:
+            self.second_sum()
+            self.third_start()
+        elif step == 3:
+            self.third_sum()
+            self.fourth_start()
+        else:
+            self.fourth_sum()
+
+
+class SmallSum:
+    def __init__(self, place, zin, cin, xin, sems, out, spread):
+        self.p, self.zin, self.cin, self.xin, self.sems = place, zin, cin, xin, sems
+        self.out, self.spread = out, spread
+        self.corner = place.d // 2
+
+    def z_copies(self):
+        p, mine = self.p, self.zin.at[self.p.z]
+        peers = (p.z_near, p.z_far, p.z_mirror)
+        return [send(mine, mine, self.sems, i, to) for i, to in enumerate(peers)]
+
+    def core_copy(self):
+        return send(self.cin.at[0], self.cin.at[1], self.sems, 3, self.p.core)
+
+    def xy_copies(self):
+        p, mine = self.p, self.xin.at[self.corner]
+        peers = (p.along_x, p.along_y, p.diagonal)
+        return [send(mine, mine, self.sems, 4 + i, to) for i, to in enumerate(peers)]
+
+    def advance(self, step):
+        cin, zin, xin = self.cin, self.zin, self.xin
+        if step == 0:
+            for copy in self.z_copies():
+                copy.start()
+        elif step == 1:
+            for copy in self.z_copies():
+                copy.wait()
+            cin[0] = self.spread(zin[0] + zin[1] + zin[2] + zin[3])
+            self.core_copy().start()
+        elif step == 2:
+            self.core_copy().wait()
+            xin[self.corner] = cin[0] + cin[1]
+            for copy in self.xy_copies():
+                copy.start()
+        else:
+            for copy in self.xy_copies():
+                copy.wait()
+            self.out[...] = xin[0] + xin[1] + xin[2] + xin[3]
 
 
 def norm_stats(v):
@@ -232,7 +296,7 @@
     T, D = r.tokens.shape
 
     barrier = pltpu.get_barrier_semaphore()
-    partners = (p.core, p.along_x, p.along_y, p.z_near, p.z_far, p.z_mirror)
+    partners = (p.core, p.along_x, p.along_y, p.diagonal, p.z_near, p.z_far, p.z_mirror)
     for partner in partners:
         pl.semaphore_signal(barrier, inc=1, device_id=partner, device_id_type=MESH)
 
@@ -241,16 +305,17 @@
     def load(src, dst, index):
         return pltpu.make_async_copy(src, dst, r.load_sems.at[index])
 
-    def slot_of(k):
-        return jnp.where(k == 2, 1, 4 + 2 * lax.rem(k, 3))
-
-    def up_load(k):
-        src = r.up_weight.at[:, pl.ds(pl.multiple_of(k * D, D), D)]
-        return load(src, pool.at[slot_of(k)], 6 + k)
-
-    def down_load(k):
-        src = r.down_weight.at[pl.ds(pl.multiple_of(k * D, D), D), :]
-        return load(src, pool.at[slot_of(k) + 1], 10 + k)
+    def chunk_of(i):
+        flip_y, flip_x = 1 - lax.rem(i, 2), 1 - i // 2
+        return 2 * (p.y + flip_y - 2 * flip_y * p.y) + p.x + flip_x - 2 * flip_x * p.x
+
+    def up_load(i):
+        src = r.up_weight.at[:, pl.ds(pl.multiple_of(chunk_of(i) * D, D), D)]
+        return load(src, pool.at[1 + i], 6 + i)
+
+    def down_load(i):
+        src = r.down_weight.at[pl.ds(pl.multiple_of(chunk_of(i) * D, D), D), :]
+        return load(src, pool.at[4 + i], 10 + i)
 
     tokens_load = load(r.tokens, r.tok, 0)
     tokens_load.start()
@@ -261,7 +326,7 @@
         qkv_loads[i].start()
     cot_load = load(r.cotangent, r.cot, 4)
     out_load = load(r.out_weight, pool.at[0], 5)
-    for copy in (cot_load, out_load, up_load(0), down_load(0), up_load(1), down_load(1)):
+    for copy in [cot_load] + [down_load(i) for i in range(4)] + [out_load]:
         copy.start()
 
     gid = r.group_ids[0]
@@ -283,81 +348,100 @@
     def nx_wait(s):
         return send(nx.at[s - 1], nx.at[s], r.nx_sems, s - 1, p.along_z(-1)).wait_recv()
 
-    kv, qT, outT, top, mass = r.kv, r.qT, r.outT, r.top, r.mass
+    kv, qT, outT, stat, mass = r.kv, r.qT, r.outT, r.stat, r.mass
+    qin, doin, stat_in = r.qin, r.doin, r.stat_in
     key_iota = lax.broadcasted_iota(jnp.int32, (T, T), 0)
     query_iota = lax.broadcasted_iota(jnp.int32, (T, T), 1)
     scale2 = HEAD**-0.5 * LOG2E
 
+    def q_copy(t):
+        src = qT if t == 0 else qin.at[t - 1]
+        return send(src, qin.at[t], r.q_sems, t, p.along_z(-1))
+
+    def q_wait(t):
+        send(qT, qin.at[t], r.q_sems, t, p.along_z(1)).wait_recv()
+
+    def q_pass(t):
+        q_wait(t)
+        q_copy(t + 1).start()
+
     def head_rows(h):
         return pl.ds(pl.multiple_of(h * HEAD, HEAD), HEAD)
 
-    def masked(s, rows):
-        scores = dot_tn(kv[s, 0, rows], qT[rows]) * scale2
-        allowed = key_iota < length - (p.z - s) * T
-        if s == 0:
+    def masked(scores, block, causal):
+        allowed = key_iota < length - block * T
+        if causal:
             allowed = allowed & (key_iota <= query_iota)
-        return jnp.where(allowed, scores, NEG_LARGE)
-
-    def attend(s):
+        return jnp.where(allowed, scores * scale2, NEG_LARGE)
+
+    def attend(s, own):
         def some_heads(g, _):
             heads = [g * GROUP + i for i in range(GROUP)]
             places = [head_rows(h) for h in heads]
-            scores = [masked(s, rows) for rows in places]
+            scores = [masked(dot_tn(kv[s, 0, rows], qT[rows]), p.z - s, own) for rows in places]
             highest = [jnp.max(v, axis=0, keepdims=True) for v in scores]
-            if s > 0:
-                highest = [jnp.maximum(v, top[h]) for v, h in zip(highest, heads)]
-                fade = [jnp.exp2(top[h] - v) for v, h in zip(highest, heads)]
+            if not own:
+                highest = [jnp.maximum(v, stat[pl.ds(h, 1)]) for v, h in zip(highest, heads)]
+                fade = [jnp.exp2(stat[pl.ds(h, 1)] - v) for v, h in zip(highest, heads)]
             weights = [jnp.exp2(v - m) for v, m in zip(scores, highest)]
             total = [column_sum(v) for v in weights]
             value = [dot(kv[s, 1, rows], v.astype(BF)) for v, rows in zip(weights, places)]
             for i, (h, rows) in enumerate(zip(heads, places)):
-                if s > 0:
-                    total[i] = total[i] + mass[h] * fade[i]
+                if not own:
+                    total[i] = total[i] + mass[pl.ds(h, 1)] * fade[i]
                     value[i] = value[i] + outT[rows] * fade[i]
-                top[h] = highest[i]
-                mass[h] = total[i]
+                stat[pl.ds(h, 1)] = highest[i]
+                mass[pl.ds(h, 1)] = total[i]
                 outT[rows] = value[i]
             return 0
 
         lax.fori_loop(0, HEADS // GROUP, some_heads, 0)
 
-    def forward_step(s):
-        if s > 0:
-            nx_wait(s)
-        if s < 3:
-            pl.when(p.z < 3)(lambda: nx_copy(s).start())
+    def project(s):
         block = nx[s]
-        nxT[:, s * T : (s + 1) * T] = block.T
-        if s == 0:
-            qkv_loads[1].wait()
         kv[s, 0] = dot(block, pool[2]).astype(BF).T
-        if s == 0:
-            qkv_loads[2].wait()
         kv[s, 1] = (dot(block, pool[3]) + r.qv_bias[1:2]).astype(BF).T
-        if s == 0:
-            qkv_loads[0].wait()
-            qT[...] = (dot(block, pool[1]) + r.qv_bias[0:1]).astype(BF).T
-        attend(s)
-
-    forward_step(0)
+
+    pl.when(p.z < 3)(lambda: nx_copy(0).start())
+    nxT[...] = nx[0].T
+    for copy in qkv_loads:
+        copy.wait()
+    qT[...] = (dot(nx[0], pool[1]) + r.qv_bias[0:1]).astype(BF).T
+    pl.when(p.z >= 1)(lambda: q_copy(0).start())
+    project(0)
+    attend(0, True)
     cot_load.wait()
     r.cotT[...] = r.cot[...].T
     for k in range(4):
         r.up_rows[k : k + 1] = r.up_bias[k * D : (k + 1) * D].reshape(1, D)
-    for s in (1, 2, 3):
-        pl.when(p.z >= s)(functools.partial(forward_step, s))
-    up_load(2).start()
-    down_load(2).start()
+
+    def act_grad(i):
+        down_load(i).wait()
+        r.act_grad[lax.rem(i, 2)] = dot_nt(r.cot[...], pool[4 + i])
+
+    lax.fori_loop(0, 2, lambda i, _: (act_grad(i), 0)[1], 0)
+
+    def earlier_block(s, _):
+        nx_wait(s)
+        pl.when((s < 3) & (p.z < 3))(lambda: nx_copy(s).start())
+        project(s)
+        attend(s, False)
+        pl.when((s == 1) & (p.z < 3))(functools.partial(q_pass, 0))
+        return 0
+
+    lax.fori_loop(1, p.z + 1, earlier_block, 0)
+    for i in (0, 1, 2):
+        up_load(i).start()
 
     def finish(h, _):
         rows = head_rows(h)
-        value = outT[rows] * (1.0 / mass[h])
+        value = outT[rows] * (1.0 / mass[pl.ds(h, 1)])
         outT[rows] = value
         r.attT[rows] = value.astype(BF)
-        top[h] = top[h] + jnp.log2(mass[h])
         return 0
 
     lax.fori_loop(0, HEADS, finish, 0, unroll=True)
+    stat[0:HEADS] = stat[0:HEADS] + jnp.log2(mass[...])
     attT = r.attT
 
     out_load.wait()
@@ -370,9 +454,9 @@
     r.total[...] = after + row_of(r.down_bias)
     r.t[...] = jnp.zeros((T, D), F32)
 
-    g_down, g_up, g_out, g_qkv = r.g_down, r.g_up, r.g_out, r.g_qkv
-
-    def scatter(name, parts):
+    g_down, g_up, g_out = r.g_down, r.g_up, r.g_out
+
+    def scatter(name, parts, out, columns=None):
         return ReduceScatter(
             p,
             getattr(r, "g_" + name),
@@ -384,13 +468,30 @@
             getattr(r, "cs_" + name),
             getattr(r, "ss_" + name),
             parts,
+            out,
+            getattr(r, "zb_" + name, None),
+            columns,
         )
 
-    down = scatter("down", "yx")
-    up = scatter("up", "z")
-    out = scatter("out", "")
-    proj = scatter("qkv", "")
-    small = r.small
+    narrow, width = D // 4, D // 2
+    down = scatter("down", "yx", r.s_down)
+    up = scatter("up", "z", r.s_up)
+    out = scatter("out", "", r.s_out, [(z * narrow, (z + 1) * narrow) for z in range(4)])
+    queries, keys, values = [(i * width, (i + 1) * width) for i in range(3)]
+    projs = [
+        scatter("p0", "", r.fin.at[0], (queries, keys, values, values)),
+        scatter("p1", "", r.fin.at[1], (queries, queries, keys, values)),
+    ]
+
+    def spread(rows):
+        table_grad = jnp.where(group_rows == gid, rows[0:1], 0.0)
+        return jnp.concatenate([table_grad, rows[1:5]], axis=0)
+
+    early = SmallSum(
+        p, r.early_z, r.early_c, r.early_x, r.early_sems, r.early_out, lambda rows: rows
+    )
+    late = SmallSum(p, r.late_z, r.late_c, r.late_x, r.late_sems, r.late_out, spread)
+    small = r.early_z.at[p.z]
     gelu_c = math.sqrt(2.0 / math.pi)
 
     def pass_on(k):
@@ -399,21 +500,21 @@
         up.core_sum(k)
         up.first_start(k)
 
-    def chunk(k, _):
+    def chunk(i, _):
+        k = chunk_of(i)
         kh, kl = k // 2, lax.rem(k, 2)
-        up_load(k).wait()
-        down_load(k).wait()
-        weight = pool[slot_of(k)]
-        weight_down = pool[slot_of(k) + 1]
+        up_load(i).wait()
+        pl.when(i >= 2)(lambda: act_grad(i))
+        weight = pool[1 + i]
+        weight_down = pool[4 + i]
         hidden = dot(r.norm_two[...], weight) + r.up_rows[pl.ds(k, 1), :]
-        act_grad = dot_nt(r.cot[...], weight_down)
         square = hidden * hidden
         th = jnp.tanh(gelu_c * hidden * (1.0 + 0.044715 * square))
         half = 0.5 + 0.5 * th
         act = (hidden * half).astype(BF)
         slope = half + 0.5 * hidden * (1.0 - th * th) * gelu_c * (1.0 + 3 * 0.044715 * square)
-        grad = act_grad * slope
-        small[pl.ds(24 + k, 1), :] = column_sum(grad)
+        grad = r.act_grad[lax.rem(i, 2)] * slope
+        small[pl.ds(4 + k, 1), :] = column_sum(grad)
         low = grad.astype(BF)
         piece = D // 2
         for cc in range(2):
@@ -424,26 +525,23 @@
                     at = z * part + h * (part // 2)
                     g_down[h, kh, kl, cc, z // 2, z % 2] = rows[at : at + part // 2]
         down.core_start(k)
-        rows = dot(r.norm_twoT[...], low).astype(BF)
         part = D // 8
-        for d in range(8):
-            for h in range(2):
-                at = d * part + h * (part // 2)
-                g_up[h, d // 4, (d // 2) % 2, d % 2, kh, kl] = rows[at : at + part // 2]
+        for y in range(2):
+            rows = dot(r.norm_twoT[y * 4 * part : (y + 1) * 4 * part], low).astype(BF)
+            for d in range(4):
+                for h in range(2):
+                    at = d * part + h * (part // 2)
+                    g_up[h, y, d // 2, d % 2, kh, kl] = rows[at : at + part // 2]
         up.core_start(k)
+        pl.when(i > 0)(lambda: pass_on(chunk_of(i - 1)))
         r.total[...] += dot(act, weight_down)
         r.t[...] += dot_nt(low, weight)
-
-        def last_load():
-            up_load(3).start()
-            down_load(3).start()
-
-        pl.when(k == 0)(last_load)
-        pl.when(k > 0)(lambda: pass_on(k - 1))
+        pl.when(i == 0)(lambda: up_load(3).start())
         return 0
 
     lax.fori_loop(0, 4, chunk, 0)
-    pass_on(3)
+    pass_on(chunk_of(3))
+    pl.when(p.z == 1)(functools.partial(q_pass, 1))
 
     qkv_loads = [
         load(r.qkv_weight.at[:, pl.ds(i * D, D)], pool.at[1 + i], 14 + i) for i in range(3)
@@ -464,198 +562,238 @@
     after_low = after_grad.astype(BF)
     doT = r.doT
     doT[...] = dot_nt(pool[0], after_low).astype(BF)
-    small[pl.ds(20, 1), :] = column_sum(after_grad)
-    small[pl.ds(21, 1), :] = column_sum(t * n)
-    small[pl.ds(22, 1), :] = column_sum(t)
-    small[pl.ds(23, 1), :] = column_sum(cot)
-    after_lowT = after_low.T
-    part = D // 8
-    for z in range(4):
-        rows = dot_nt(attT[...], after_lowT[z * (D // 4) : (z + 1) * (D // 4)]).astype(BF)
-        for d in range(8):
-            for h in range(2):
-                at = d * part + h * (part // 2)
-                g_out[h, d // 4, (d // 2) % 2, d % 2, z // 2, z % 2] = rows[at : at + part // 2]
-    out.core_start(0)
-
-    delta = r.delta
     for h in range(HEADS):
         rows = slice(h * HEAD, (h + 1) * HEAD)
-        delta[h] = column_sum(doT[rows].astype(F32) * outT[rows])
+        stat[HEADS + h : HEADS + h + 1] = column_sum(doT[rows].astype(F32) * outT[rows])
+    def group_rows_of(group):
+        return pl.ds(pl.multiple_of(group * width, width), width)
+
+    def do_copy(t, group):
+        rows = group_rows_of(group)
+        src = doT.at[rows] if isinstance(t, int) and t == 0 else doin.at[t - 1, rows]
+        return send(src, doin.at[t, rows], r.do_sems, 2 * t + group, p.along_z(-1))
+
+    def stat_copy(t):
+        src = stat if isinstance(t, int) and t == 0 else stat_in.at[t - 1]
+        return send(src, stat_in.at[t], r.stat_sems, t, p.along_z(-1))
+
+    def do_send(t, group):
+        pl.when(group == 0)(lambda: stat_copy(t).start())
+        do_copy(t, group).start()
+
+    def stat_wait(t):
+        send(stat, stat_in.at[t], r.stat_sems, t, p.along_z(1)).wait_recv()
+
+    def do_wait(t, group):
+        rows = group_rows_of(group)
+        send(doT.at[rows], doin.at[t, rows], r.do_sems, 2 * t + group, p.along_z(1)).wait_recv()
+        pl.when(group == 0)(lambda: stat_wait(t))
+
+    for group in range(2):
+        pl.when(p.z >= 1)(functools.partial(do_send, 0, group))
+    small[pl.ds(0, 1), :] = column_sum(after_grad)
+    small[pl.ds(1, 1), :] = column_sum(t * n)
+    small[pl.ds(2, 1), :] = column_sum(t)
+    small[pl.ds(3, 1), :] = column_sum(cot)
+    rows = dot(attT[...], after_low).astype(BF)
+    part = D // 8
+    for d in range(8):
+        for h in range(2):
+            at = d * part + h * (part // 2)
+            g_out[h, d // 4, (d // 2) % 2, d % 2] = rows[at : at + part // 2]
+    out.core_start(0)
+
     outT[...] = jnp.zeros((D, T), F32)
-    mg = r.mg
-
-    def attend_back(s):
-        lanes = slice(s * T, (s + 1) * T)
-
-        def some_heads(g, _):
-            heads = [g * GROUP + i for i in range(GROUP)]
-            places = [head_rows(h) for h in heads]
-            scores = [masked(s, rows) for rows in places]
-            prob_grad = [dot_tn(kv[s, 1, rows], doT[rows]) for rows in places]
-            probs = [jnp.exp2(v - top[h]) for v, h in zip(scores, heads)]
-            score_grad = [
-                (v * (w - delta[h])).astype(BF) for v, w, h in zip(probs, prob_grad, heads)
-            ]
+    key_grad, value_grad = r.key_grad, r.value_grad
+    mixed = (kv.at[1, 0], kv.at[1, 1], kv.at[2, 0])
+
+    def grads_of(s, group, queries, out_grads, sums, causal, for_queries, for_keys):
+        heads = [group * GROUP + i for i in range(GROUP)]
+        places = [head_rows(h) for h in heads]
+        scores = [dot_tn(kv[s, 0, rows], queries[rows]) for rows in places]
+        prob_grad = [dot_tn(kv[s, 1, rows], out_grads[rows]) for rows in places]
+        scores = [masked(v, p.z - s, causal) for v in scores]
+        probs = [jnp.exp2(v - sums[pl.ds(h, 1)]) for v, h in zip(scores, heads)]
+        score_grad = [
+            (v * (w - sums[pl.ds(HEADS + h, 1)])).astype(BF)
+            for v, w, h in zip(probs, prob_grad, heads)
+        ]
+        if for_queries:
+            query_add = [dot(kv[s, 0, rows], v) for v, rows in zip(score_grad, places)]
+        if for_keys:
             probs = [v.astype(BF) for v in probs]
-            query_add = [dot(kv[s, 0, rows], v) for v, rows in zip(score_grad, places)]
-            key_add = [dot_nt(qT[rows], v) for v, rows in zip(score_grad, places)]
-            value_add = [dot_nt(doT[rows], v) for v, rows in zip(probs, places)]
-            for i, rows in enumerate(places):
+            key_add = [dot_nt(queries[rows], v) for v, rows in zip(score_grad, places)]
+            value_add = [dot_nt(out_grads[rows], v) for v, rows in zip(probs, places)]
+        for i, rows in enumerate(places):
+            if for_queries:
                 outT[rows] = outT[rows] + query_add[i]
-                mg[0, rows, lanes] = (key_add[i] * HEAD**-0.5).astype(BF)
-                mg[1, rows, lanes] = value_add[i].astype(BF)
-            return 0
-
-        lax.fori_loop(0, HEADS // GROUP, some_heads, 0)
-
-    def t1_of(s):
-        lanes = slice(s * T, (s + 1) * T)
-        return dot(pool[2], mg[0, :, lanes]) + dot(pool[3], mg[1, :, lanes])
-
-    def t1_copy(s):
-        return send(kv.at[s, 0], r.t1_in.at[s - 1], r.t1_sems, s - 1, p.along_z(-1))
-
-    def t1_wait(s):
-        send(kv.at[s + 1, 0], r.t1_in.at[s], r.t1_sems, s, p.along_z(1)).wait_recv()
-
-    def back_step(s):
-        attend_back(s)
-        kv[s, 0] = t1_of(s).astype(BF)
-        pl.when(p.z == 3)(lambda: t1_copy(s).start())
-
-    def no_step(s):
-        lanes = slice(s * T, (s + 1) * T)
-        nxT[:, lanes] = jnp.zeros((D, T), BF)
-        for i in range(2):
-            mg[i, :, lanes] = jnp.zeros((D, T), BF)
+            if for_keys and for_queries:
+                key_grad[rows] = key_add[i]
+                value_grad[rows] = value_add[i]
+            elif for_keys:
+                key_grad[rows] = key_grad[rows] + key_add[i]
+                value_grad[rows] = value_grad[rows] + value_add[i]
+
+    def query_step(i, _):
+        grads_of(p.z - i // 2, lax.rem(i, 2), qT, doT, stat, False, True, False)
+        return 0
+
+    def own_step(group, _):
+        grads_of(0, group, qT, doT, stat, True, True, True)
+        return 0
+
+    def key_step(t, group):
+        pl.when((p.z == 0) & (group == 0))(lambda: q_wait(t))
+        do_wait(t, group)
+        pl.when(p.z >= 1)(lambda: do_send(t + 1, group))
+        grads_of(0, group, qin.at[t], doin.at[t], stat_in.at[t], False, False, True)
+
+    def proj_grad(group):
+        rows = slice(group * width, (group + 1) * width)
+        mixed[0][rows] = (outT[rows] * HEAD**-0.5).astype(BF)
+        mixed[1][rows] = (key_grad[rows] * HEAD**-0.5).astype(BF)
+        mixed[2][rows] = value_grad[rows].astype(BF)
+        target = (r.g_p0, r.g_p1)[group]
+        part = D // 8
+        for i in range(3):
+            piece = dot_nt(nxT[...], mixed[i][rows]).astype(BF)
+            for d in range(8):
+                for h in range(2):
+                    at = d * part + h * (part // 2)
+                    target[h, d // 4, (d // 2) % 2, d % 2, :, i * width : (i + 1) * width] = piece[
+                        at : at + part // 2
+                    ]
+        projs[group].core_start(0)
+
+    def norm_back_one():
+        outT[...] = sum(dot(pool[1 + i], mixed[i][...]) for i in range(3))
+        ones = jnp.ones((8, T), BF)
+        rows = r.late_z.at[p.z]
+        rows[pl.ds(3, 1), :] = dot_nt(ones, mixed[0][...])[0:1]
+        rows[pl.ds(4, 1), :] = dot_nt(ones, mixed[2][...])[0:1]
+        t1 = outT[...].T
+        start = r.tok[...].astype(F32) + table_row
+        mean, inverse = norm_stats(start)
+        n = (start - mean) * inverse
+        start_grad = r.after[...] + norm_back(t1, row_of(r.first_gain), n, inverse)
+        r.norm_two[...] = start_grad.astype(BF)
+        tokens_store.start()
+        rows[pl.ds(0, 1), :] = column_sum(start_grad)
+        rows[pl.ds(1, 1), :] = column_sum(t1 * n)
+        rows[pl.ds(2, 1), :] = column_sum(t1)
+        late.advance(0)
+
+    tokens_store = pltpu.make_async_copy(r.norm_two, r.grad_tokens, r.load_sems.at[18])
 
     for copy in qkv_loads:
         copy.wait()
-    for s in (3, 2, 1):
-        pl.when(p.z >= s)(functools.partial(back_step, s))
-        pl.when(p.z < s)(functools.partial(no_step, s))
-        if s == 3:
-            out.core_sum(0)
-            out.first_start(0)
-    attend_back(0)
-
-    query_grad = outT[...] * HEAD**-0.5
-    query_low = query_grad.astype(BF)
-    share = 3 * D // 4
-    part = D // 8
-    for z in range(4):
-        columns = []
-        for i in range(3):
-            low_at, high_at = max(z * share, i * D) - i * D, min((z + 1) * share, (i + 1) * D) - i * D
-            if low_at >= high_at:
-                continue
-            if i == 0:
-                columns.append(dot_nt(nxT[:, 0:T], query_low[low_at:high_at]))
-            else:
-                columns.append(dot_nt(nxT[...], mg[i - 1, low_at:high_at]))
-        rows = (columns[0] if len(columns) == 1 else jnp.concatenate(columns, axis=1)).astype(BF)
-        for d in range(8):
-            for h in range(2):
-                at = d * part + h * (part // 2)
-                g_qkv[h, d // 4, (d // 2) % 2, d % 2, z // 2, z % 2] = rows[at : at + part // 2]
-    proj.core_start(0)
-    t1 = t1_of(0) + dot(pool[1], query_low)
-    r.outT[...] = t1
-    ones = jnp.ones((8, 4 * T), BF)
-    small[pl.ds(18, 1), :] = dot_nt(ones[:, 0:T], query_low)[0:1]
-    small[pl.ds(19, 1), :] = dot_nt(ones, mg[1])[0:1]
-
-    down.first_sum()
-    down.second_start()
-    proj.core_sum(0)
-    proj.first_start(0)
-
-    def t1_pass(s):
-        t1_wait(s)
-        kv[s, 0] = kv[s, 0] + r.t1_in[s]
-        t1_copy(s).start()
-
-    pl.when(p.z == 2)(lambda: t1_pass(2))
-    up.first_sum()
-    up.second_start()
-    out.first_sum()
-    out.second_start()
-    pl.when((p.z >= 1) & (p.z < 3))(lambda: t1_pass(1))
-    down.second_sum()
-    down.third_start()
-    up.second_sum()
-    up.third_start()
-
-    def t1_last():
-        t1_wait(0)
-        outT[...] = outT[...] + r.t1_in[0].astype(F32)
-
-    pl.when(p.z < 3)(t1_last)
-    t1 = outT[...].T
-    start = r.tok[...].astype(F32) + table_row
-    mean, inverse = norm_stats(start)
-    n = (start - mean) * inverse
-    start_grad = r.after[...] + norm_back(t1, row_of(r.first_gain), n, inverse)
-    r.norm_two[...] = start_grad.astype(BF)
-    tokens_store = pltpu.make_async_copy(r.norm_two, r.grad_tokens, r.load_sems.at[18])
-    tokens_store.start()
-    small[pl.ds(0, 16), :] = jnp.where(group_rows == gid, column_sum(start_grad), 0.0)
-    small[pl.ds(16, 1), :] = column_sum(t1 * n)
-    small[pl.ds(17, 1), :] = column_sum(t1)
-
-    small_in, small_sems = r.small_in, r.small_sems
-    small_to = [p.core, p.along_x, p.along_y, p.z_near, p.z_far]
-
-    def small_copy(step):
-        return send(small, small_in.at[step], small_sems, step, small_to[step])
-
-    def small_sum(step):
-        small_copy(step).wait()
-        small[...] = small[...] + small_in[step]
-
-    small_copy(0).start()
-    out.second_sum()
-    out.third_start()
-    down.third_sum()
-    down.fourth_start()
-    small_sum(0)
-    small_copy(1).start()
-    proj.first_sum()
-    proj.second_start()
-    up.third_sum()
-    up.fourth_start()
-    small_sum(1)
-    small_copy(2).start()
-    out.third_sum()
-    out.fourth_start()
-    small_sum(2)
-    small_copy(3).start()
-    proj.second_sum()
-    proj.third_start()
-    small_sum(3)
-    small_copy(4).start()
-    down.fourth_sum(r.s_down)
-    up.fourth_sum(r.s_up)
-    out.fourth_sum(r.s_out)
-    proj.third_sum()
-    proj.fourth_start()
-    small_sum(4)
-    r.small_out[...] = small[...]
+    lax.fori_loop(0, 2 * p.z, query_step, 0)
+    lax.fori_loop(0, 2, own_step, 0)
+    step = functools.partial
+
+    ahead = (
+        (
+            (0, step(early.advance, 0)),
+            (3, step(down.advance, 1)),
+            (3, step(down.advance, 2)),
+            (3, step(up.advance, 1)),
+            (5, step(proj_grad, 0)),
+        ),
+        (
+            (0, step(down.advance, 1)),
+            (3, step(proj_grad, 0)),
+        ),
+        (
+        ),
+        (
+        ),
+    )
+    rest = (
+        ((), step(proj_grad, 1)),
+        ((0, 1), step(down.advance, 1)),
+        ((0, 1), step(proj_grad, 0)),
+        ((0,), step(up.advance, 1)),
+        ((), step(projs[0].advance, 0)),
+        ((0,), step(early.advance, 0)),
+        ((), norm_back_one),
+        ((0,), step(down.advance, 2)),
+        ((), step(projs[1].advance, 0)),
+        ((), step(up.advance, 2)),
+        ((), step(down.advance, 3)),
+        ((), step(projs[0].advance, 1)),
+        ((), step(projs[1].advance, 1)),
+        ((), step(up.advance, 3)),
+        ((), step(projs[0].advance, 2)),
+        ((), step(out.advance, 0)),
+        ((), step(projs[1].advance, 2)),
+        ((), step(out.advance, 1)),
+        ((), step(down.advance, 4)),
+        ((), step(projs[0].advance, 3)),
+        ((), step(early.advance, 1)),
+        ((), step(late.advance, 1)),
+        ((), step(out.advance, 2)),
+        ((), step(late.advance, 2)),
+        ((), step(projs[1].advance, 3)),
+        ((), step(early.advance, 2)),
+        ((), step(out.advance, 3)),
+        ((), step(up.advance, 4)),
+        ((), step(projs[1].advance, 4)),
+        ((), step(late.advance, 3)),
+        ((), step(projs[0].advance, 4)),
+        ((), step(early.advance, 3)),
+        ((), step(out.advance, 4)),
+    )
+
+    def half_round(i, _):
+        for z in range(3):
+            for at, one in ahead[z]:
+                pl.when((p.z == z) & (i == at))(one)
+        pl.when(p.z + i // 2 < 3)(lambda: key_step(i // 2, lax.rem(i, 2)))
+        return 0
+
+    for _, one in ahead[3]:
+        pl.when(p.z == 3)(one)
+    lax.fori_loop(0, 7, half_round, 0)
+    for done, one in rest:
+        if len(done) == 0:
+            one()
+        else:
+            planes = [z for z in range(4) if z not in done]
+            if planes:
+                pl.when(functools.reduce(jnp.logical_or, [p.z == z for z in planes]))(one)
     for s in (0, 1, 2):
         pl.when((p.z < 3) & (p.z >= s))(lambda s=s: nx_copy(s).wait_send())
-    for s in (1, 2, 3):
-        pl.when(p.z >= s)(lambda s=s: t1_copy(s).wait_send())
+    def sent(t):
+        q_copy(t).wait_send()
+        stat_copy(t).wait_send()
+        do_copy(t, 0).wait_send()
+        do_copy(t, 1).wait_send()
+
+    for t in range(3):
+        pl.when((p.z >= 1) & (p.z + t <= 3))(functools.partial(sent, t))
     result_store.wait()
     tokens_store.wait()
-    proj.fourth_sum(r.s_qkv)
+    fin = r.fin
+    layouts = (
+        ((0, 0, width), (1, 0, narrow)),
+        ((1, narrow, width), (0, 0, width)),
+        ((1, 0, width), (0, 0, narrow)),
+        ((0, narrow, width), (1, 0, width)),
+    )
+
+    def lay_out(order):
+        for h in range(2):
+            r.s_qkv[h] = jnp.concatenate([fin[g, h, :, a:b] for g, a, b in order], axis=1)
+
+    for z in range(4):
+        pl.when(p.z == z)(functools.partial(lay_out, layouts[z]))
 
 
 def row_of(ref):
     return ref[...].reshape(1, ref.shape[0])
 
 
-def outputs_kernel(result, grad_tokens, small, s_qkv, s_out, s_up, s_down, *outs):
+def outputs_kernel(result, grad_tokens, early, late, s_qkv, s_out, s_up, s_down, *outs):
     (
         o_result,
         o_tokens,
@@ -673,22 +811,19 @@
         o_down,
         o_down_bias,
     ) = outs
-    D = small.shape[1]
+    D = early.shape[1]
     o_result[...] = result[...].reshape(o_result.shape)
     o_tokens[...] = grad_tokens[...].reshape(o_tokens.shape)
-    o_table[...] = small[0:16]
-    o_qv_bias[...] = small[18:20]
-    for ref, row in (
-        (o_first_gain, 16),
-        (o_first_shift, 17),
-        (o_out_bias, 20),
-        (o_second_gain, 21),
-        (o_second_shift, 22),
-        (o_down_bias, 23),
-    ):
-        ref[...] = small[row]
+    o_table[...] = late[0:16]
+    o_first_gain[...] = late[16]
+    o_first_shift[...] = late[17]
+    o_out_bias[...] = early[0]
+    o_second_gain[...] = early[1]
+    o_second_shift[...] = early[2]
+    o_down_bias[...] = early[3]
     for k in range(4):
-        o_up_bias[pl.ds(k * D, D)] = small[24 + k]
+        o_up_bias[pl.ds(k * D, D)] = early[4 + k]
+    o_qv_bias[...] = late[18:20]
     for ref, value in ((o_qkv, s_qkv), (o_out, s_out), (o_up, s_up), (o_down, s_down)):
         half = value.shape[1]
         for h in range(2):
@@ -747,7 +882,8 @@
     outputs = dict(
         result=((T, D), BF),
         grad_tokens=((T, D), BF),
-        small_out=((28, D), F32),
+        early_out=((8, D), F32),
+        late_out=((20, D), F32),
     )
     outputs.update({"s_" + k: ((2,) + shares[k], F32) for k in ("qkv", "out", "up", "down")})
     dma = pltpu.SemaphoreType.DMA
@@ -757,41 +893,63 @@
         cot=pltpu.VMEM((T, D), BF),
         cotT=pltpu.VMEM((D, T), BF),
         nx=pltpu.VMEM((4, T, D), BF),
-        nxT=pltpu.VMEM((D, 4 * T), BF),
+        nxT=pltpu.VMEM((D, T), BF),
         qT=pltpu.VMEM((D, T), BF),
         kv=pltpu.VMEM((4, 2, D, T), BF),
         outT=pltpu.VMEM((D, T), F32),
-        top=pltpu.VMEM((HEADS, 1, T), F32),
-        mass=pltpu.VMEM((HEADS, 1, T), F32),
-        delta=pltpu.VMEM((HEADS, 1, T), F32),
+        stat=pltpu.VMEM((2 * HEADS, T), F32),
+        mass=pltpu.VMEM((HEADS, T), F32),
+        qin=pltpu.VMEM((3, D, T), BF),
+        doin=pltpu.VMEM((3, D, T), BF),
+        stat_in=pltpu.VMEM((3, 2 * HEADS, T), F32),
+        key_grad=pltpu.VMEM((D, T), F32),
+        value_grad=pltpu.VMEM((D, T), F32),
         attT=pltpu.VMEM((D, T), BF),
         after=pltpu.VMEM((T, D), F32),
         norm_two=pltpu.VMEM((T, D), BF),
         norm_twoT=pltpu.VMEM((D, T), BF),
+        act_grad=pltpu.VMEM((2, T, D), F32),
         total=pltpu.VMEM((T, D), F32),
         t=pltpu.VMEM((T, D), F32),
         doT=pltpu.VMEM((D, T), BF),
-        mg=pltpu.VMEM((2, D, 4 * T), BF),
-        t1_in=pltpu.VMEM((3, D, T), BF),
         up_rows=pltpu.VMEM((4, D), F32),
-        small=pltpu.VMEM((28, D), F32),
-        small_in=pltpu.VMEM((5, 28, D), F32),
+        early_z=pltpu.VMEM((4, 8, D), F32),
+        early_c=pltpu.VMEM((2, 8, D), F32),
+        early_x=pltpu.VMEM((4, 8, D), F32),
+        late_z=pltpu.VMEM((4, 5, D), F32),
+        late_c=pltpu.VMEM((2, 20, D), F32),
+        late_x=pltpu.VMEM((4, 20, D), F32),
+        fin=pltpu.VMEM((2, 2, D // 16, D // 2), F32),
         load_sems=dma((19,)),
         nx_sems=dma((2, 3)),
-        t1_sems=dma((2, 3)),
-        small_sems=dma((2, 5)),
-    )
-    for name, (rows, columns) in shares.items():
+        q_sems=dma((2, 3)),
+        do_sems=dma((2, 6)),
+        stat_sems=dma((2, 3)),
+        early_sems=dma((2, 7)),
+        late_sems=dma((2, 7)),
+    )
+    places = dict(
+        down=(2, 2, D // 8, F // 8),
+        up=(2, 2, D // 16, F // 4),
+        out=(D // 16, D),
+        p0=(D // 16, 3 * D // 2),
+        p1=(D // 16, 3 * D // 2),
+    )
+    columns_of = dict(shares, p0=(D // 16, D // 2), p1=(D // 16, D // 2))
+    for name, place in places.items():
+        rows, columns = columns_of[name]
         extra = {
-            "g_" + name: pltpu.VMEM((2, 2, 2, 2, 2, 2, rows, columns), BF),
-            "rc_" + name: pltpu.VMEM((2, 2, 2, 2, 2, rows, columns), BF),
-            "r1_" + name: pltpu.VMEM((2, 2, 2, 2, rows, columns), BF),
-            "r2_" + name: pltpu.VMEM((2, 2, 2, rows, columns), BF),
+            "g_" + name: pltpu.VMEM((2, 2, 2, 2) + place, BF),
+            "rc_" + name: pltpu.VMEM((2, 2, 2) + place, BF),
+            "r1_" + name: pltpu.VMEM((2, 2) + place, BF),
+            "r2_" + name: pltpu.VMEM((2,) + place, BF),
             "rz1_" + name: pltpu.VMEM((2, 2, rows, columns), BF),
             "rz2_" + name: pltpu.VMEM((2, rows, columns), BF),
             "cs_" + name: dma((2, 4)),
             "ss_" + name: dma((2, 12)),
         }
+        if len(place) == 2:
+            extra["zb_" + name] = pltpu.VMEM((2, 2, 2, rows, columns), BF)
         scratch.update(extra)
     names = list(inputs) + list(outputs) + list(scratch)
     done = pl.pallas_call(

time: 137 us -> 121 us (0.88)
  Pallas kernels: 135 us -> 119 us
    pallas_call x1, Pallas kernels: 132 us -> 116 us  [fused(): pl.pallas_call(functools.partial(layer_kernel, names), name='layer', out_...]
where the time goes in v3:
time: 121 us
  Pallas kernels  119 us (98%)
  between operations  2.11 us (2%)
    pallas_call x1, Pallas kernels, fused(): pl.pallas_call(functools.partial(layer_kernel, names), name='layer', out_...  116 us
    pallas_call x1, Pallas kernels, fused(): pl.pallas_call(outputs_kernel, name='outputs', out_shape=[shape((1, T, D)...  2.71 us

profile of v3, /device:TPU:0, one launch (start us, length us, event | category | flops | bytes accessed | tf_op | source)
XLA Modules:
  0.0 120.6 jit_solution(4900497134808819871)
XLA Ops:
  1.9 115.8 %layer.1 = (bf16[256,768]{1,0:T(8,128)(2,1)}, bf16[256,768]{1,0:T(8,128)(2,1)}, f32[8,768]{1,0:T(8,128)}, f32[20,768]{1,0:T(8,128)}, f32[2,48,576]{2,1,0:T(8,128...) custom-call(bf16[256,768]{1,0:T(8,128)(2,1)} %bitcast.3, s32[1]{0:T(128)S(6)} %copy.32.refs_1_, ...), custom_call_target="tpu_custom_call" | custom-call | tf_op jit(solution)/shard_map/layer/pallas_call | solution.py:955
  117.8 2.7 %outputs.1 = (bf16[1,256,768]{2,1,0:T(8,128)(2,1)}, bf16[1,256,768]{2,1,0:T(8,128)(2,1)}, f32[16,768]{1,0:T(8,128)}, f32[768]{0:T(1024)}, f32[768]{0:T(1024)}, /...) custom-call(bf16[256,768]{1,0:T(8,128)(2,1)} %get-tuple-element.38.r, ...), custom_call_target="tpu_custom_call" | custom-call | tf_op jit(solution)/shard_map/outputs/pallas_call | solution.py:967

commit v4 on v3

--- a/solution.py
+++ b/solution.py
@@ -23,6 +23,17 @@
 
 
 BF = jnp.bfloat16
+VECTORS = (
+    "group_table",
+    "first_gain",
+    "first_shift",
+    "qv_bias",
+    "out_bias",
+    "second_gain",
+    "second_shift",
+    "up_bias",
+    "down_bias",
+)
 F32 = jnp.float32
 MESH = pl.DeviceIdType.MESH
 LOG2E = 1.4426950408889634
@@ -213,7 +224,11 @@
         p, zb = self.p, self.zb
         self.fourth_copy().wait()
         for h in range(2):
-            self.out[h] = zb[h, p.zh, p.zl].astype(F32) + self.rz2[h].astype(F32)
+            total = zb[h, p.zh, p.zl].astype(F32) + self.rz2[h].astype(F32)
+            if callable(self.out):
+                self.out(h, total)
+            else:
+                self.out[h] = total
 
     def advance(self, step):
         if step == 0:
@@ -319,6 +334,11 @@
 
     tokens_load = load(r.tokens, r.tok, 0)
     tokens_load.start()
+    vectors = [
+        load(getattr(r, name), getattr(r, "v_" + name), 20 + i) for i, name in enumerate(VECTORS)
+    ]
+    for copy in vectors:
+        copy.start()
     qkv_loads = [
         load(r.qkv_weight.at[:, pl.ds(i * D, D)], pool.at[1 + i], 1 + i) for i in range(3)
     ]
@@ -331,22 +351,30 @@
 
     gid = r.group_ids[0]
     length = r.lengths[0]
-    table = r.group_table[...]
+    for copy in vectors:
+        copy.wait()
+    table = r.v_group_table[...]
     group_rows = lax.broadcasted_iota(jnp.int32, table.shape, 0)
     table_row = jnp.sum(jnp.where(group_rows == gid, table, 0.0), axis=0, keepdims=True)
     tokens_load.wait()
     start = r.tok[...].astype(F32) + table_row
     mean, inverse = norm_stats(start)
     nx, nxT = r.nx, r.nxT
-    nx[0] = ((start - mean) * inverse * row_of(r.first_gain) + row_of(r.first_shift)).astype(BF)
+    r.norm_two[...] = ((start - mean) * inverse * row_of(r.v_first_gain) + row_of(r.v_first_shift)).astype(BF)
 
     pl.semaphore_wait(barrier, len(partners))
 
-    def nx_copy(s):
-        return send(nx.at[s], nx.at[s + 1], r.nx_sems, s, p.along_z(1))
-
-    def nx_wait(s):
-        return send(nx.at[s - 1], nx.at[s], r.nx_sems, s - 1, p.along_z(-1)).wait_recv()
+    def nx_copy(s, half):
+        rows = pl.ds(half * (T // 2), T // 2)
+        own = isinstance(s, int) and s == 0
+        src = r.norm_two.at[rows] if own else nx.at[s - 1, rows]
+        return send(src, nx.at[s, rows], r.nx_sems, 2 * s + half, p.along_z(1))
+
+    def nx_pass(s, half):
+        rows = pl.ds(half * (T // 2), T // 2)
+        here = nx.at[s - 1, rows]
+        send(here, here, r.nx_sems, 2 * (s - 1) + half, p.along_z(-1)).wait_recv()
+        pl.when((s < 3) & (p.z < 3))(lambda: nx_copy(s, half).start())
 
     kv, qT, outT, stat, mass = r.kv, r.qT, r.outT, r.stat, r.mass
     qin, doin, stat_in = r.qin, r.doin, r.stat_in
@@ -397,23 +425,23 @@
 
         lax.fori_loop(0, HEADS // GROUP, some_heads, 0)
 
-    def project(s):
-        block = nx[s]
+    def project(s, block):
         kv[s, 0] = dot(block, pool[2]).astype(BF).T
-        kv[s, 1] = (dot(block, pool[3]) + r.qv_bias[1:2]).astype(BF).T
-
-    pl.when(p.z < 3)(lambda: nx_copy(0).start())
-    nxT[...] = nx[0].T
+        kv[s, 1] = (dot(block, pool[3]) + r.v_qv_bias[1:2]).astype(BF).T
+
+    for half in range(2):
+        pl.when(p.z < 3)(functools.partial(lambda half: nx_copy(0, half).start(), half))
+    nxT[...] = r.norm_two[...].T
     for copy in qkv_loads:
         copy.wait()
-    qT[...] = (dot(nx[0], pool[1]) + r.qv_bias[0:1]).astype(BF).T
+    qT[...] = (dot(r.norm_two[...], pool[1]) + r.v_qv_bias[0:1]).astype(BF).T
     pl.when(p.z >= 1)(lambda: q_copy(0).start())
-    project(0)
+    project(0, r.norm_two[...])
     attend(0, True)
     cot_load.wait()
     r.cotT[...] = r.cot[...].T
     for k in range(4):
-        r.up_rows[k : k + 1] = r.up_bias[k * D : (k + 1) * D].reshape(1, D)
+        r.up_rows[k : k + 1] = r.v_up_bias[k * D : (k + 1) * D].reshape(1, D)
 
     def act_grad(i):
         down_load(i).wait()
@@ -422,9 +450,9 @@
     lax.fori_loop(0, 2, lambda i, _: (act_grad(i), 0)[1], 0)
 
     def earlier_block(s, _):
-        nx_wait(s)
-        pl.when((s < 3) & (p.z < 3))(lambda: nx_copy(s).start())
-        project(s)
+        nx_pass(s, 0)
+        nx_pass(s, 1)
+        project(s, nx[s - 1])
         attend(s, False)
         pl.when((s == 1) & (p.z < 3))(functools.partial(q_pass, 0))
         return 0
@@ -445,13 +473,15 @@
     attT = r.attT
 
     out_load.wait()
-    after = r.tok[...].astype(F32) + table_row + dot(attT[...].T, pool[0]) + row_of(r.out_bias)
+    after = r.tok[...].astype(F32) + table_row + dot(attT[...].T, pool[0]) + row_of(r.v_out_bias)
     r.after[...] = after
     mean, inverse = norm_stats(after)
-    norm_two = ((after - mean) * inverse * row_of(r.second_gain) + row_of(r.second_shift)).astype(BF)
+    norm_two = ((after - mean) * inverse * row_of(r.v_second_gain) + row_of(r.v_second_shift)).astype(BF)
+    for half in range(2):
+        pl.when(p.z < 3)(functools.partial(lambda half: nx_copy(0, half).wait_send(), half))
     r.norm_two[...] = norm_two
     r.norm_twoT[...] = norm_two.T
-    r.total[...] = after + row_of(r.down_bias)
+    r.total[...] = after + row_of(r.v_down_bias)
     r.t[...] = jnp.zeros((T, D), F32)
 
     g_down, g_up, g_out = r.g_down, r.g_up, r.g_out
@@ -479,9 +509,22 @@
     out = scatter("out", "", r.s_out, [(z * narrow, (z + 1) * narrow) for z in range(4)])
     queries, keys, values = [(i * width, (i + 1) * width) for i in range(3)]
     projs = [
-        scatter("p0", "", r.fin.at[0], (queries, keys, values, values)),
-        scatter("p1", "", r.fin.at[1], (queries, queries, keys, values)),
+        scatter("p0", "", lambda h, v: lay_out(0, h, v), (queries, keys, values, values)),
+        scatter("p1", "", lambda h, v: lay_out(1, h, v), (queries, queries, keys, values)),
     ]
+    layouts = (
+        ((0, width, 0), (0, width, narrow), (0, narrow, width), (narrow, width, 0)),
+        ((0, narrow, width), (narrow, width, 0), (0, width, 0), (0, width, narrow)),
+    )
+
+    def lay_out(chunk, h, value):
+        for z, (first, last, at) in enumerate(layouts[chunk]):
+
+            def store(first=first, last=last, at=at):
+                r.s_qkv[h, :, at : at + last - first] = value[:, first:last]
+
+            pl.when(p.z == z)(store)
+
 
     def spread(rows):
         table_grad = jnp.where(group_rows == gid, rows[0:1], 0.0)
@@ -549,15 +592,15 @@
     for copy in qkv_loads:
         copy.start()
 
-    nx[3] = r.total[...].astype(BF)
-    result_store = pltpu.make_async_copy(nx.at[3], r.result, r.load_sems.at[17])
+    nx[2] = r.total[...].astype(BF)
+    result_store = pltpu.make_async_copy(nx.at[2], r.result, r.load_sems.at[17])
     result_store.start()
     cot = r.cot[...].astype(F32)
     after = r.after[...]
     mean, inverse = norm_stats(after)
     n = (after - mean) * inverse
     t = r.t[...]
-    after_grad = cot + norm_back(t, row_of(r.second_gain), n, inverse)
+    after_grad = cot + norm_back(t, row_of(r.v_second_gain), n, inverse)
     r.after[...] = after_grad
     after_low = after_grad.astype(BF)
     doT = r.doT
@@ -675,7 +718,7 @@
         start = r.tok[...].astype(F32) + table_row
         mean, inverse = norm_stats(start)
         n = (start - mean) * inverse
-        start_grad = r.after[...] + norm_back(t1, row_of(r.first_gain), n, inverse)
+        start_grad = r.after[...] + norm_back(t1, row_of(r.v_first_gain), n, inverse)
         r.norm_two[...] = start_grad.astype(BF)
         tokens_store.start()
         rows[pl.ds(0, 1), :] = column_sum(start_grad)
@@ -761,8 +804,9 @@
             planes = [z for z in range(4) if z not in done]
             if planes:
                 pl.when(functools.reduce(jnp.logical_or, [p.z == z for z in planes]))(one)
-    for s in (0, 1, 2):
-        pl.when((p.z < 3) & (p.z >= s))(lambda s=s: nx_copy(s).wait_send())
+    for s in (1, 2):
+        for half in range(2):
+            pl.when((p.z < 3) & (p.z >= s))(lambda s=s, half=half: nx_copy(s, half).wait_send())
     def sent(t):
         q_copy(t).wait_send()
         stat_copy(t).wait_send()
@@ -773,21 +817,6 @@
         pl.when((p.z >= 1) & (p.z + t <= 3))(functools.partial(sent, t))
     result_store.wait()
     tokens_store.wait()
-    fin = r.fin
-    layouts = (
-        ((0, 0, width), (1, 0, narrow)),
-        ((1, narrow, width), (0, 0, width)),
-        ((1, 0, width), (0, 0, narrow)),
-        ((0, narrow, width), (1, 0, width)),
-    )
-
-    def lay_out(order):
-        for h in range(2):
-            r.s_qkv[h] = jnp.concatenate([fin[g, h, :, a:b] for g, a, b in order], axis=1)
-
-    for z in range(4):
-        pl.when(p.z == z)(functools.partial(lay_out, layouts[z]))
-
 
 def row_of(ref):
     return ref[...].reshape(1, ref.shape[0])
@@ -859,19 +888,19 @@
         group_ids=(group_ids, smem),
         lengths=(lengths, smem),
         cotangent=(cotangent.reshape(T, D), any_spec),
-        group_table=(group_table, vmem),
-        first_gain=(first_gain, vmem),
-        first_shift=(first_shift, vmem),
+        group_table=(group_table, any_spec),
+        first_gain=(first_gain, any_spec),
+        first_shift=(first_shift, any_spec),
         qkv_weight=(qkv_weight, any_spec),
-        qv_bias=(query_value_bias, vmem),
+        qv_bias=(query_value_bias, any_spec),
         out_weight=(out_weight, any_spec),
-        out_bias=(out_bias, vmem),
-        second_gain=(second_gain, vmem),
-        second_shift=(second_shift, vmem),
+        out_bias=(out_bias, any_spec),
+        second_gain=(second_gain, any_spec),
+        second_shift=(second_shift, any_spec),
         up_weight=(up_weight, any_spec),
-        up_bias=(up_bias, vmem),
+        up_bias=(up_bias, any_spec),
         down_weight=(down_weight, any_spec),
-        down_bias=(down_bias, vmem),
+        down_bias=(down_bias, any_spec),
     )
     shares = dict(
         down=(D // 8, F // 8),
@@ -889,10 +918,19 @@
     dma = pltpu.SemaphoreType.DMA
     scratch = dict(
         pool=pltpu.VMEM((8, D, D), BF),
+        v_group_table=pltpu.VMEM(group_table.shape, F32),
+        v_first_gain=pltpu.VMEM((D,), F32),
+        v_first_shift=pltpu.VMEM((D,), F32),
+        v_qv_bias=pltpu.VMEM((2, D), F32),
+        v_out_bias=pltpu.VMEM((D,), F32),
+        v_second_gain=pltpu.VMEM((D,), F32),
+        v_second_shift=pltpu.VMEM((D,), F32),
+        v_up_bias=pltpu.VMEM((F,), F32),
+        v_down_bias=pltpu.VMEM((D,), F32),
         tok=pltpu.VMEM((T, D), BF),
         cot=pltpu.VMEM((T, D), BF),
         cotT=pltpu.VMEM((D, T), BF),
-        nx=pltpu.VMEM((4, T, D), BF),
+        nx=pltpu.VMEM((3, T, D), BF),
         nxT=pltpu.VMEM((D, T), BF),
         qT=pltpu.VMEM((D, T), BF),
         kv=pltpu.VMEM((4, 2, D, T), BF),
@@ -919,9 +957,8 @@
         late_z=pltpu.VMEM((4, 5, D), F32),
         late_c=pltpu.VMEM((2, 20, D), F32),
         late_x=pltpu.VMEM((4, 20, D), F32),
-        fin=pltpu.VMEM((2, 2, D // 16, D // 2), F32),
-        load_sems=dma((19,)),
-        nx_sems=dma((2, 3)),
+        load_sems=dma((29,)),
+        nx_sems=dma((2, 6)),
         q_sems=dma((2, 3)),
         do_sems=dma((2, 6)),
         stat_sems=dma((2, 3)),

time: 121 us -> 118 us (0.975)
  Pallas kernels: 119 us -> 116 us
    pallas_call x1, Pallas kernels: 116 us -> 113 us  [fused(): pl.pallas_call(functools.partial(layer_kernel, names), name='layer', out_...]
where the time goes in v4:
time: 118 us
  Pallas kernels  116 us (98%)
  between operations  2.11 us (2%)
    pallas_call x1, Pallas kernels, fused(): pl.pallas_call(functools.partial(layer_kernel, names), name='layer', out_...  113 us
    pallas_call x1, Pallas kernels, fused(): pl.pallas_call(outputs_kernel, name='outputs', out_shape=[shape((1, T, D)...  2.71 us

profile of v4, /device:TPU:0, one launch (start us, length us, event | category | flops | bytes accessed | tf_op | source)
XLA Modules:
  0.0 117.7 jit_solution(4435216723673987015)
XLA Ops:
  1.9 112.9 %layer.1 = (bf16[256,768]{1,0:T(8,128)(2,1)}, bf16[256,768]{1,0:T(8,128)(2,1)}, f32[8,768]{1,0:T(8,128)}, f32[20,768]{1,0:T(8,128)}, f32[2,48,576]{2,1,0:T(8,128...) custom-call(bf16[256,768]{1,0:T(8,128)(2,1)} %bitcast.3, s32[1]{0:T(128)S(6)} %copy.32.refs_1_, ...), custom_call_target="tpu_custom_call" | custom-call | tf_op jit(solution)/shard_map/layer/pallas_call | solution.py:992
  114.8 2.7 %outputs.1 = (bf16[1,256,768]{2,1,0:T(8,128)(2,1)}, bf16[1,256,768]{2,1,0:T(8,128)(2,1)}, f32[16,768]{1,0:T(8,128)}, f32[768]{0:T(1024)}, f32[768]{0:T(1024)}, /...) custom-call(bf16[256,768]{1,0:T(8,128)(2,1)} %get-tuple-element.38.r, ...), custom_call_target="tpu_custom_call" | custom-call | tf_op jit(solution)/shard_map/outputs/pallas_call | solution.py:1004

commit v5 on v4

--- a/solution.py
+++ b/solution.py
@@ -425,9 +425,9 @@
 
         lax.fori_loop(0, HEADS // GROUP, some_heads, 0)
 
-    def project(s, block):
-        kv[s, 0] = dot(block, pool[2]).astype(BF).T
-        kv[s, 1] = (dot(block, pool[3]) + r.v_qv_bias[1:2]).astype(BF).T
+    def project(s, block, rows):
+        kv[s, 0, :, rows] = dot(block, pool[2]).astype(BF).T
+        kv[s, 1, :, rows] = (dot(block, pool[3]) + r.v_qv_bias[1:2]).astype(BF).T
 
     for half in range(2):
         pl.when(p.z < 3)(functools.partial(lambda half: nx_copy(0, half).start(), half))
@@ -436,7 +436,7 @@
         copy.wait()
     qT[...] = (dot(r.norm_two[...], pool[1]) + r.v_qv_bias[0:1]).astype(BF).T
     pl.when(p.z >= 1)(lambda: q_copy(0).start())
-    project(0, r.norm_two[...])
+    project(0, r.norm_two[...], slice(0, T))
     attend(0, True)
     cot_load.wait()
     r.cotT[...] = r.cot[...].T
@@ -450,9 +450,10 @@
     lax.fori_loop(0, 2, lambda i, _: (act_grad(i), 0)[1], 0)
 
     def earlier_block(s, _):
-        nx_pass(s, 0)
-        nx_pass(s, 1)
-        project(s, nx[s - 1])
+        for half in range(2):
+            nx_pass(s, half)
+            rows = slice(half * (T // 2), (half + 1) * (T // 2))
+            project(s, nx[s - 1, rows], rows)
         attend(s, False)
         pl.when((s == 1) & (p.z < 3))(functools.partial(q_pass, 0))
         return 0
@@ -736,15 +737,14 @@
 
     ahead = (
         (
-            (0, step(early.advance, 0)),
-            (3, step(down.advance, 1)),
+            (1, step(up.advance, 1)),
+            (1, step(down.advance, 1)),
+            (3, step(out.advance, 0)),
             (3, step(down.advance, 2)),
-            (3, step(up.advance, 1)),
             (5, step(proj_grad, 0)),
         ),
         (
-            (0, step(down.advance, 1)),
-            (3, step(proj_grad, 0)),
+            (2, step(down.advance, 1)),
         ),
         (
         ),
@@ -752,38 +752,38 @@
         ),
     )
     rest = (
+        ((0, 1), step(down.advance, 1)),
+        ((0,), step(up.advance, 1)),
+        ((), step(early.advance, 0)),
+        ((0,), step(proj_grad, 0)),
+        ((0,), step(down.advance, 2)),
+        ((), step(projs[0].advance, 0)),
         ((), step(proj_grad, 1)),
-        ((0, 1), step(down.advance, 1)),
-        ((0, 1), step(proj_grad, 0)),
-        ((0,), step(up.advance, 1)),
-        ((), step(projs[0].advance, 0)),
-        ((0,), step(early.advance, 0)),
+        ((), step(up.advance, 2)),
+        ((), step(projs[1].advance, 0)),
         ((), norm_back_one),
-        ((0,), step(down.advance, 2)),
-        ((), step(projs[1].advance, 0)),
-        ((), step(up.advance, 2)),
+        ((), step(projs[0].advance, 1)),
         ((), step(down.advance, 3)),
-        ((), step(projs[0].advance, 1)),
+        ((), step(early.advance, 1)),
         ((), step(projs[1].advance, 1)),
+        ((0,), step(out.advance, 0)),
         ((), step(up.advance, 3)),
+        ((), step(early.advance, 2)),
         ((), step(projs[0].advance, 2)),
-        ((), step(out.advance, 0)),
+        ((), step(late.advance, 1)),
         ((), step(projs[1].advance, 2)),
+        ((), step(down.advance, 4)),
         ((), step(out.advance, 1)),
-        ((), step(down.advance, 4)),
         ((), step(projs[0].advance, 3)),
-        ((), step(early.advance, 1)),
-        ((), step(late.advance, 1)),
+        ((), step(late.advance, 2)),
         ((), step(out.advance, 2)),
-        ((), step(late.advance, 2)),
         ((), step(projs[1].advance, 3)),
-        ((), step(early.advance, 2)),
+        ((), step(early.advance, 3)),
+        ((), step(late.advance, 3)),
+        ((), step(up.advance, 4)),
         ((), step(out.advance, 3)),
-        ((), step(up.advance, 4)),
         ((), step(projs[1].advance, 4)),
-        ((), step(late.advance, 3)),
         ((), step(projs[0].advance, 4)),
-        ((), step(early.advance, 3)),
         ((), step(out.advance, 4)),
     )
 

time: 118 us -> 117 us (level)
  no operation moved by 1% of the time
where the time goes in v5:
time: 117 us
  Pallas kernels  115 us (98%)
  between operations  2.11 us (2%)
    pallas_call x1, Pallas kernels, fused(): pl.pallas_call(functools.partial(layer_kernel, names), name='layer', out_...  112 us
    pallas_call x1, Pallas kernels, fused(): pl.pallas_call(outputs_kernel, name='outputs', out_shape=[shape((1, T, D)...  2.71 us

profile of v5, /device:TPU:0, one launch (start us, length us, event | category | flops | bytes accessed | tf_op | source)
XLA Modules:
  0.0 117.3 jit_solution(18117901667969337299)
XLA Ops:
  1.9 112.4 %layer.1 = (bf16[256,768]{1,0:T(8,128)(2,1)}, bf16[256,768]{1,0:T(8,128)(2,1)}, f32[8,768]{1,0:T(8,128)}, f32[20,768]{1,0:T(8,128)}, f32[2,48,576]{2,1,0:T(8,128...) custom-call(bf16[256,768]{1,0:T(8,128)(2,1)} %bitcast.3, s32[1]{0:T(128)S(6)} %copy.32.refs_1_, ...), custom_call_target="tpu_custom_call" | custom-call | tf_op jit(solution)/shard_map/layer/pallas_call | solution.py:992
  114.4 2.7 %outputs.1 = (bf16[1,256,768]{2,1,0:T(8,128)(2,1)}, bf16[1,256,768]{2,1,0:T(8,128)(2,1)}, f32[16,768]{1,0:T(8,128)}, f32[768]{0:T(1024)}, f32[768]{0:T(1024)}, /...) custom-call(bf16[256,768]{1,0:T(8,128)(2,1)} %get-tuple-element.38.r, ...), custom_call_target="tpu_custom_call" | custom-call | tf_op jit(solution)/shard_map/outputs/pallas_call | solution.py:1004

commit v6 on v5

--- a/solution.py
+++ b/solution.py
@@ -23,6 +23,7 @@
 
 
 BF = jnp.bfloat16
+RESULTS = ("early_out", "late_out", "s_qkv", "s_out", "s_up", "s_down")
 VECTORS = (
     "group_table",
     "first_gain",
@@ -228,7 +229,9 @@
             if callable(self.out):
                 self.out(h, total)
             else:
-                self.out[h] = total
+                self.out[0][h] = total
+        if not callable(self.out):
+            self.out[1].start()
 
     def advance(self, step):
         if step == 0:
@@ -284,7 +287,8 @@
         else:
             for copy in self.xy_copies():
                 copy.wait()
-            self.out[...] = xin[0] + xin[1] + xin[2] + xin[3]
+            self.out[0][...] = xin[0] + xin[1] + xin[2] + xin[3]
+            self.out[1].start()
 
 
 def norm_stats(v):
@@ -504,10 +508,20 @@
             columns,
         )
 
+    stores = {
+        name: pltpu.make_async_copy(
+            getattr(r, "o_" + name), getattr(r, name), r.store_sems.at[i]
+        )
+        for i, name in enumerate(RESULTS)
+    }
+
+    def result_of(name):
+        return getattr(r, "o_" + name), stores[name]
+
     narrow, width = D // 4, D // 2
-    down = scatter("down", "yx", r.s_down)
-    up = scatter("up", "z", r.s_up)
-    out = scatter("out", "", r.s_out, [(z * narrow, (z + 1) * narrow) for z in range(4)])
+    down = scatter("down", "yx", result_of("s_down"))
+    up = scatter("up", "z", result_of("s_up"))
+    out = scatter("out", "", result_of("s_out"), [(z * narrow, (z + 1) * narrow) for z in range(4)])
     queries, keys, values = [(i * width, (i + 1) * width) for i in range(3)]
     projs = [
         scatter("p0", "", lambda h, v: lay_out(0, h, v), (queries, keys, values, values)),
@@ -522,7 +536,7 @@
         for z, (first, last, at) in enumerate(layouts[chunk]):
 
             def store(first=first, last=last, at=at):
-                r.s_qkv[h, :, at : at + last - first] = value[:, first:last]
+                r.o_s_qkv[h, :, at : at + last - first] = value[:, first:last]
 
             pl.when(p.z == z)(store)
 
@@ -532,9 +546,9 @@
         return jnp.concatenate([table_grad, rows[1:5]], axis=0)
 
     early = SmallSum(
-        p, r.early_z, r.early_c, r.early_x, r.early_sems, r.early_out, lambda rows: rows
-    )
-    late = SmallSum(p, r.late_z, r.late_c, r.late_x, r.late_sems, r.late_out, spread)
+        p, r.early_z, r.early_c, r.early_x, r.early_sems, result_of("early_out"), lambda rows: rows
+    )
+    late = SmallSum(p, r.late_z, r.late_c, r.late_x, r.late_sems, result_of("late_out"), spread)
     small = r.early_z.at[p.z]
     gelu_c = math.sqrt(2.0 / math.pi)
 
@@ -815,8 +829,11 @@
 
     for t in range(3):
         pl.when((p.z >= 1) & (p.z + t <= 3))(functools.partial(sent, t))
+    stores["s_qkv"].start()
     result_store.wait()
     tokens_store.wait()
+    for copy in stores.values():
+        copy.wait()
 
 def row_of(ref):
     return ref[...].reshape(1, ref.shape[0])
@@ -988,13 +1005,15 @@
         if len(place) == 2:
             extra["zb_" + name] = pltpu.VMEM((2, 2, 2, rows, columns), BF)
         scratch.update(extra)
+    scratch.update({"o_" + name: pltpu.VMEM(*outputs[name]) for name in RESULTS})
+    scratch["store_sems"] = dma((len(RESULTS),))
     names = list(inputs) + list(outputs) + list(scratch)
     done = pl.pallas_call(
         functools.partial(layer_kernel, names),
         name="layer",
         out_shape=[jax.ShapeDtypeStruct(*o) for o in outputs.values()],
         in_specs=[i[1] for i in inputs.values()],
-        out_specs=[any_spec] * 2 + [vmem] * (len(outputs) - 2),
+        out_specs=[any_spec] * len(outputs),
         scratch_shapes=list(scratch.values()),
         compiler_params=pltpu.CompilerParams(
             collective_id=0, has_side_effects=True, vmem_limit_bytes=VMEM_LIMIT

time: 117 us -> 117 us (level)
  no operation moved by 1% of the time
where the time goes in v6:
time: 117 us
  Pallas kernels  115 us (98%)
  between operations  2.11 us (2%)
    pallas_call x1, Pallas kernels, fused(): pl.pallas_call(functools.partial(layer_kernel, names), name='layer', out_...  112 us
    pallas_call x1, Pallas kernels, fused(): pl.pallas_call(outputs_kernel, name='outputs', out_shape=[shape((1, T, D)...  2.71 us

profile of v6, /device:TPU:0, one launch (start us, length us, event | category | flops | bytes accessed | tf_op | source)
XLA Modules:
  0.0 117.1 jit_solution(14779931426343464382)
XLA Ops:
  1.9 112.3 %layer.1 = (bf16[256,768]{1,0:T(8,128)(2,1)}, bf16[256,768]{1,0:T(8,128)(2,1)}, f32[8,768]{1,0:T(8,128)}, f32[20,768]{1,0:T(8,128)}, f32[2,48,576]{2,1,0:T(8,128...) custom-call(bf16[256,768]{1,0:T(8,128)(2,1)} %bitcast.3, s32[1]{0:T(128)S(6)} %copy.32.refs_1_, ...), custom_call_target="tpu_custom_call" | custom-call | tf_op jit(solution)/shard_map/layer/pallas_call | solution.py:1011
  114.2 2.7 %outputs.1 = (bf16[1,256,768]{2,1,0:T(8,128)(2,1)}, bf16[1,256,768]{2,1,0:T(8,128)(2,1)}, f32[16,768]{1,0:T(8,128)}, f32[768]{0:T(1024)}, f32[768]{0:T(1024)}, /...) custom-call(bf16[256,768]{1,0:T(8,128)(2,1)} %get-tuple-element.38.r, ...), custom_call_target="tpu_custom_call" | custom-call | tf_op jit(solution)/shard_map/outputs/pallas_call | solution.py:1023

commit v7 on v5

--- a/solution.py
+++ b/solution.py
@@ -445,9 +445,9 @@
 
     def act_grad(i):
         down_load(i).wait()
-        r.act_grad[lax.rem(i, 2)] = dot_nt(r.cot[...], pool[4 + i])
-
-    lax.fori_loop(0, 2, lambda i, _: (act_grad(i), 0)[1], 0)
+        r.act_grad[lax.rem(i, 3)] = dot_nt(r.cot[...], pool[4 + i])
+
+    lax.fori_loop(0, 3, lambda i, _: (act_grad(i), 0)[1], 0)
 
     def earlier_block(s, _):
         for half in range(2):
@@ -548,7 +548,7 @@
         k = chunk_of(i)
         kh, kl = k // 2, lax.rem(k, 2)
         up_load(i).wait()
-        pl.when(i >= 2)(lambda: act_grad(i))
+        pl.when(i >= 3)(lambda: act_grad(i))
         weight = pool[1 + i]
         weight_down = pool[4 + i]
         hidden = dot(r.norm_two[...], weight) + r.up_rows[pl.ds(k, 1), :]
@@ -557,7 +557,7 @@
         half = 0.5 + 0.5 * th
         act = (hidden * half).astype(BF)
         slope = half + 0.5 * hidden * (1.0 - th * th) * gelu_c * (1.0 + 3 * 0.044715 * square)
-        grad = r.act_grad[lax.rem(i, 2)] * slope
+        grad = r.act_grad[lax.rem(i, 3)] * slope
         small[pl.ds(4 + k, 1), :] = column_sum(grad)
         low = grad.astype(BF)
         piece = D // 2
@@ -946,7 +946,7 @@
         after=pltpu.VMEM((T, D), F32),
         norm_two=pltpu.VMEM((T, D), BF),
         norm_twoT=pltpu.VMEM((D, T), BF),
-        act_grad=pltpu.VMEM((2, T, D), F32),
+        act_grad=pltpu.VMEM((3, T, D), F32),
         total=pltpu.VMEM((T, D), F32),
         t=pltpu.VMEM((T, D), F32),
         doT=pltpu.VMEM((D, T), BF),

time: 117 us -> 118 us (level)
  no operation moved by 1% of the time
where the time goes in v7:
time: 118 us; the launch traced here: 117 us
  Pallas kernels  115 us (97%)
  between operations  2.11 us (2%)
    pallas_call x1, Pallas kernels, fused(): pl.pallas_call(functools.partial(layer_kernel, names), name='layer', out_...  113 us
    pallas_call x1, Pallas kernels, fused(): pl.pallas_call(outputs_kernel, name='outputs', out_shape=[shape((1, T, D)...  2.71 us

profile of v7, /device:TPU:0, one launch (start us, length us, event | category | flops | bytes accessed | tf_op | source)
XLA Modules:
  0.0 117.4 jit_solution(14040133486170583270)
XLA Ops:
  1.9 112.5 %layer.1 = (bf16[256,768]{1,0:T(8,128)(2,1)}, bf16[256,768]{1,0:T(8,128)(2,1)}, f32[8,768]{1,0:T(8,128)}, f32[20,768]{1,0:T(8,128)}, f32[2,48,576]{2,1,0:T(8,128...) custom-call(bf16[256,768]{1,0:T(8,128)(2,1)} %bitcast.3, s32[1]{0:T(128)S(6)} %copy.32.refs_1_, ...), custom_call_target="tpu_custom_call" | custom-call | tf_op jit(solution)/shard_map/layer/pallas_call | solution.py:992
  114.5 2.7 %outputs.1 = (bf16[1,256,768]{2,1,0:T(8,128)(2,1)}, bf16[1,256,768]{2,1,0:T(8,128)(2,1)}, f32[16,768]{1,0:T(8,128)}, f32[768]{0:T(1024)}, f32[768]{0:T(1024)}, /...) custom-call(bf16[256,768]{1,0:T(8,128)(2,1)} %get-tuple-element.38.r, ...), custom_call_target="tpu_custom_call" | custom-call | tf_op jit(solution)/shard_map/outputs/pallas_call | solution.py:1004
